TPU v7x, 256 devices: a whole 4x4x8 slice. The times are simulated.
256 devices in a mesh: row: 8 (over y, x_hi), col: 32 (over z, x_lo, core).
Axes of the slice: x: 4 (x_hi: 2, x_lo: 2; x = x_hi * 2 + x_lo), y: 4, z: 8, core: 2. Of those that a mesh axis runs over, the one named last changes fastest.
Arguments:
- tokens: bfloat16 [3072, 5120], P('col', 'row'), may hold values from -6 to 6
- up_blocks: bfloat16 [8, 32, 30, 4096], P('row', 'col'), may hold values from -0.21875 to 0.21875
- up_layout: int32 [8, 32, 30], P('row', 'col'), may hold values from 0 to 99, as said below
- up_counts: int32 [8, 32], P('row', 'col'), may hold values from 1 to 30, as said below
- down_blocks: bfloat16 [8, 32, 30, 4096], P('row', 'col'), may hold values from -0.109375 to 0.109375
- down_layout: int32 [8, 32, 30], P('row', 'col'), may hold values from 0 to 99, as said below
- down_counts: int32 [8, 32], P('row', 'col'), may hold values from 1 to 30, as said below
- grad_out: bfloat16 [3072, 5120], P('col', 'row'), may hold values from -6 to 6
Outputs:
- grad_tokens: bfloat16 [3072, 5120], P('col', 'row')
- up_grad: float32 [8, 32, 30, 4096], P('row', 'col')
- down_grad: float32 [8, 32, 30, 4096], P('row', 'col')
Inputs may be any that keep to these rules, and one draw needn't show every extreme that they name: `up_layout`: the 30 entries of one tile are distinct tile-local block numbers; number id stands for block row id // 10 and block column id % 10 of the tile. `down_layout`: the 30 entries of one tile are distinct tile-local block numbers; number id stands for hidden block id % 10 and model-width block id // 10 of the tile. `up_counts`: some tile has all 30 slots live. `down_counts`: some tile has all 30 slots live.
All inputs are finite; a program needn't handle non-finite values.
Results may differ from a plain program's by a relative error of at most 0.0049.
Values may be sent and summed in bfloat16 or wider, within the bound.
A program may use at most 192 MiB of HBM per device.

v0:
```python
import math

import jax
import jax.numpy as jnp
from jax import lax
from jax.sharding import PartitionSpec as P

FF = 20480
BLOCK = 64


GELU_C = 0.7978845608028654
GELU_A = 0.044715


def gelu_value(values):
    return 0.5 * values * (1.0 + jnp.tanh(GELU_C * (values + GELU_A * values * values * values)))


def gelu_slope(values):
    tanh_part = jnp.tanh(GELU_C * (values + GELU_A * values * values * values))
    return 0.5 * (1.0 + tanh_part) + 0.5 * values * (1.0 - tanh_part * tanh_part) * GELU_C * (
        1.0 + 3.0 * GELU_A * values * values
    )


def block_size(length):
    return math.gcd(length, 512)


def tile_term(source, blocks, pick_ids, put_ids, live_mask, put_count, transpose):
    block_width = blocks.shape[-1]
    shaped = source.reshape(source.shape[0], source.shape[1] // block_width, block_width)
    chosen = jnp.take(shaped, pick_ids, axis=1)
    einsum_form = "tsn,skn->tsk" if transpose else "tsk,skn->tsn"
    products = jnp.einsum(einsum_form, chosen, blocks, preferred_element_type=jnp.float32)
    targets = jnp.arange(put_count, dtype=jnp.int32)
    placement = ((put_ids[:, None] == targets[None, :]) & live_mask[:, None]).astype(jnp.float32)
    result = jnp.einsum("tsn,sf->tfn", products, placement, precision=lax.Precision.HIGHEST)
    return result.reshape(result.shape[0], put_count * block_width)


def by_blocks(function, source):
    block_rows = block_size(source.shape[0])
    number = source.shape[0] // block_rows
    stacked = source.reshape(number, block_rows, source.shape[1])
    result = lax.map(function, stacked)
    return result.reshape(number * block_rows, result.shape[2])


def grad_blocks(left_all, right_all, pick_left, pick_right, live_mask, block_width):
    block_rows = block_size(left_all.shape[0])
    number = left_all.shape[0] // block_rows
    left_stack = left_all.reshape(number, block_rows, left_all.shape[1] // block_width, block_width)
    right_stack = right_all.reshape(
        number, block_rows, right_all.shape[1] // block_width, block_width
    )

    def add_block(running, pieces):
        left_sel = jnp.take(pieces[0], pick_left, axis=1)
        right_sel = jnp.take(pieces[1], pick_right, axis=1)
        return (
            running
            + jnp.einsum("tsk,tsn->skn", left_sel, right_sel, preferred_element_type=jnp.float32),
            None,
        )

    empty = jnp.zeros((pick_left.shape[0], block_width, block_width), jnp.float32)
    running, _ = lax.scan(add_block, empty, (left_stack, right_stack))
    return running * live_mask[:, None, None].astype(jnp.float32)


def body(tokens, up_blocks, up_layout, up_counts, down_blocks, down_layout, down_counts, grad_out):
    block_width = BLOCK
    up_ids = up_layout[0, 0]
    down_ids = down_layout[0, 0]
    slot_count = up_ids.shape[0]
    slot_ids = jnp.arange(slot_count, dtype=jnp.int32)
    up_live = slot_ids < up_counts[0, 0]
    down_live = slot_ids < down_counts[0, 0]
    d_blocks = tokens.shape[1] // block_width
    f_blocks = FF // block_width // lax.axis_size("col")
    up_tile = up_blocks[0, 0].reshape(slot_count, block_width, block_width)
    down_tile = down_blocks[0, 0].reshape(slot_count, block_width, block_width)
    tokens_all = lax.all_gather(tokens, "col", axis=0, tiled=True)
    grad_all = lax.all_gather(grad_out, "col", axis=0, tiled=True)
    pre_part = by_blocks(
        lambda rows_in: tile_term(
            rows_in, up_tile, up_ids // f_blocks, up_ids % f_blocks, up_live, f_blocks, False
        ),
        tokens_all,
    )
    hidden_part = by_blocks(
        lambda rows_in: tile_term(
            rows_in, down_tile, down_ids // f_blocks, down_ids % f_blocks, down_live, f_blocks, True
        ),
        grad_all,
    )
    pre, hidden_grad = (
        lax.psum_scatter(pre_part, "row", scatter_dimension=0, tiled=True),
        lax.psum_scatter(hidden_part, "row", scatter_dimension=0, tiled=True),
    )
    hidden_share = gelu_value(pre).astype(jnp.bfloat16)
    grad_share = (hidden_grad * gelu_slope(pre)).astype(jnp.bfloat16)
    hidden_all, pre_grad_all = (
        lax.all_gather(hidden_share, "row", axis=0, tiled=True),
        lax.all_gather(grad_share, "row", axis=0, tiled=True),
    )
    up_grad = grad_blocks(
        tokens_all, pre_grad_all, up_ids // f_blocks, up_ids % f_blocks, up_live, block_width
    )
    down_grad = grad_blocks(
        hidden_all, grad_all, down_ids % f_blocks, down_ids // f_blocks, down_live, block_width
    )
    input_total = lax.psum_scatter(
        by_blocks(
            lambda rows_in: tile_term(
                rows_in, up_tile, up_ids % f_blocks, up_ids // f_blocks, up_live, d_blocks, True
            ),
            pre_grad_all,
        ),
        "col",
        scatter_dimension=0,
        tiled=True,
    )
    up_flat = up_grad.reshape(slot_count, block_width * block_width)
    down_flat = down_grad.reshape(slot_count, block_width * block_width)
    return (input_total.astype(jnp.bfloat16), up_flat[None, None], down_flat[None, None])


def solution(mesh):
    in_specs = (
        P("col", "row"),
        P("row", "col", None, None),
        P("row", "col", None),
        P("row", "col"),
        P("row", "col", None, None),
        P("row", "col", None),
        P("row", "col"),
        P("col", "row"),
    )
    out_specs = (P("col", "row"), P("row", "col", None, None), P("row", "col", None, None))
    return jax.shard_map(body, mesh=mesh, in_specs=in_specs, out_specs=out_specs, check_vma=False)
```

profile of v0, /device:TPU:24, one launch (start us, length us, event | category | flops | bytes accessed | tf_op | source)
XLA Modules:
  0.0 682.1 jit_solution(1181645104295555364)
XLA Ops:
  12.4 67.2 %all-gather.7.cloned.1.call-done = bf16[3072,640]{1,0:T(8,128)(2,1)} async-done(((bf16[96,640]{1,0:T(8,128)(2,1)}), bf16[3072,640]{1,0:T(8,128)(2,1)}) %all-gather.7.cloned.1.call-update) | async-done | bytes 3932176 | tf_op jit(solution)/shard_map/all_gather | solution.py:85
  79.6 3.6 broadcast.179.clone2
  83.2 64.5 %while.62 = (s32[]{:T(128)}, f32[6,512,640]{2,1,0:T(8,128)}, s32[30]{0:T(128)S(1)}, bf16[6,512,640]{2,1,0:T(8,128)(2,1)}, s32[30]{0:T(128)S(1)}, /*index=5*/bf16[30,64,64]{1,2,0:T(8,128)(2,1)}, s32[]{:T(128)}, s32[]{:T(128)}) while((s32[]{:T(128)}, f32[6,512,640]{2,1,0:T(8,128)}, s32[30]{0:T(128)S(1)}, ...), condition=%wide.region_4.6_spmd.clone, body=%wide.region_3.5_spmd.clone.sunk | while | flops 244779200 | bytes 25810580 | solution.py:47
  87.7 3.8 fusion.121
  98.4 3.8 fusion.121
  109.2 3.8 fusion.121
  120.0 3.8 fusion.121
  130.7 3.8 fusion.121
  141.5 3.8 fusion.121
  150.5 3.6 broadcast.179.clone2.1
  154.1 64.5 %while.61 = (s32[]{:T(128)}, f32[6,512,640]{2,1,0:T(8,128)}, s32[30]{0:T(128)S(1)}, bf16[6,512,640]{2,1,0:T(8,128)(2,1)}, s32[30]{0:T(128)S(1)}, /*index=5*/bf16[30,64,64]{2,1,0:T(8,128)(2,1)}, s32[]{:T(128)}, s32[]{:T(128)}) while((s32[]{:T(128)}, f32[6,512,640]{2,1,0:T(8,128)}, s32[30]{0:T(128)S(1)}, ...), condition=%wide.region_1.3_spmd.clone, body=%wide.region_0.2_spmd.clone.sunk | while | flops 244779200 | bytes 25810580 | solution.py:47
  158.6 3.8 fusion.116
  169.3 3.8 fusion.116
  180.1 3.8 fusion.116
  190.8 3.8 fusion.116
  201.6 3.8 fusion.116
  212.3 3.8 fusion.116
  218.6 47.9 %reduce-scatter.6.cloned.1.call-done = f32[384,640]{1,0:T(8,128)} async-done(((f32[3072,640]{1,0:T(8,128)}), f32[384,640]{1,0:T(8,128)}) %reduce-scatter.6.cloned.1.call-update) | async-done | bytes 983056 | tf_op jit(solution)/shard_map/reduce_scatter | solution.py:100
  266.5 118.8 %reduce-scatter.4.cloned.1.call-done = f32[384,640]{1,0:T(8,128)} async-done(((f32[3072,640]{1,0:T(8,128)}), f32[384,640]{1,0:T(8,128)}) %reduce-scatter.4.cloned.1.call-update) | async-done | bytes 983056 | tf_op jit(solution)/shard_map/reduce_scatter | solution.py:101
  390.5 6.3 copy.34
  396.8 8.8 %reshape.135 = bf16[6,512,10,64]{1,0,3,2:T(8,128)(2,1)} reshape(bf16[3072,640]{0,1:T(8,128)(2,1)} %copy.34) | data formatting | bytes 7864320 | tf_op jit(solution)/shard_map/reshape | solution.py:54
  405.6 5.8 copy.36
  411.3 6.3 copy.39
  417.6 8.7 %reshape.138 = bf16[6,512,10,64]{1,0,3,2:T(8,128)(2,1)} reshape(bf16[3072,640]{0,1:T(8,128)(2,1)} %copy.39) | data formatting | bytes 7864320 | tf_op jit(solution)/shard_map/reshape | solution.py:55
  426.4 6.0 copy.41
  432.4 8.7 %reduce-scatter.8.cloned.1.call-start = ((), (), s32[]{:S(2)}) async-start(), calls=%async_computation.8 | async-start | bytes 8110080 | tf_op jit(solution)/shard_map/reduce_scatter | solution.py:115
  441.1 19.4 %all-gather.9.cloned.1.call-done = bf16[3072,640]{1,0:T(8,128)(2,1)} async-done(((bf16[384,640]{1,0:T(8,128)(2,1)}), bf16[3072,640]{1,0:T(8,128)(2,1)}) %all-gather.9.cloned.1.call-update) | async-done | bytes 3932176 | tf_op jit(solution)/shard_map/all_gather | solution.py:107
  460.5 6.3 copy.35
  466.9 8.7 %reshape.136 = bf16[6,512,10,64]{1,0,3,2:T(8,128)(2,1)} reshape(bf16[3072,640]{0,1:T(8,128)(2,1)} %copy.35) | data formatting | bytes 7864320 | tf_op jit(solution)/shard_map/reshape | solution.py:55
  475.6 6.1 copy.37
  481.7 3.7 broadcast.179.clone
  485.4 58.3 %while.63 = (s32[]{:T(128)}, f32[6,512,640]{2,1,0:T(8,128)}, s32[30,1]{0,1:T(1,128)S(1)}, s32[30]{0:T(128)S(1)}, bf16[6,512,640]{2,1,0:T(8,128)(2,1)}, /*index=5...) while((s32[]{:T(128)}, f32[6,512,640]{2,1,0:T(8,128)}, s32[30,1]{0,1:T(1,128)S(1)}, ...), condition=%wide.region_7.9_spmd.clone, body=%wide.region_6.8_spmd.clone.sunk | while | flops 244779184 | bytes 25810580 | solution.py:47
  488.9 3.8 fusion.127
  498.7 3.8 fusion.127
  508.3 3.8 fusion.127
  518.1 3.8 fusion.127
  527.8 3.8 fusion.127
  537.5 3.8 fusion.127
  544.4 45.5 %while.64 = (s32[]{:T(128)}, f32[30,64,64]{2,1,0:T(8,128)}, bf16[6,512,10,64]{1,3,2,0:T(8,128)(2,1)}, s32[30]{0:T(128)S(1)}, bf16[6,512,10,64]{1,3,2,0:T(8,128)(2,1)}, /*index=5*/s32[30]{0:T(128)S(1)}, s32[]{:T(128)}, s32[]{:T(128)}) while((s32[]{:T(128)}, f32[30,64,64]{2,1,0:T(8,128)}, bf16[6,512,10,64]{1,3,2,0:T(8,128)(2,1)}, ...), condition=%wide.region_10.12_spmd.clone, body=%wide.region_9.11_spmd.clone.sunk | while | flops 128043552 | bytes 15410571 | solution.py:69
  563.5 3.5 fusion.130
  571.1 3.5 fusion.130
  578.8 3.5 fusion.130
  592.7 6.3 copy.38
  599.0 8.7 %reshape.137 = bf16[6,512,10,64]{1,0,3,2:T(8,128)(2,1)} reshape(bf16[3072,640]{0,1:T(8,128)(2,1)} %copy.38) | data formatting | bytes 7864320 | tf_op jit(solution)/shard_map/reshape | solution.py:54
  607.7 5.8 copy.40
  613.5 45.7 %while.65 = (s32[]{:T(128)}, f32[30,64,64]{2,1,0:T(8,128)}, bf16[6,512,10,64]{1,3,2,0:T(8,128)(2,1)}, s32[30]{0:T(128)S(1)}, bf16[6,512,10,64]{1,3,2,0:T(8,128)(2,1)}, /*index=5*/s32[30]{0:T(128)S(1)}, s32[]{:T(128)}, s32[]{:T(128)}) while((s32[]{:T(128)}, f32[30,64,64]{2,1,0:T(8,128)}, bf16[6,512,10,64]{1,3,2,0:T(8,128)(2,1)}, ...), condition=%wide.region_12.14_spmd.clone, body=%wide.region_11.13_spmd.clone.sunk | while | flops 128043552 | bytes 15410571 | solution.py:69
  648.0 3.5 fusion.133
  661.9 11.5 %reduce-scatter.8.cloned.1.call-done = f32[96,640]{1,0:T(8,128)} async-done(((f32[3072,640]{1,0:T(8,128)}), f32[96,640]{1,0:T(8,128)}) %reduce-scatter.8.cloned.1.call-update) | async-done | bytes 245776 | tf_op jit(solution)/shard_map/reduce_scatter | solution.py:115
  (319 shorter events, 213.4 us)
Async XLA Ops:
  7.2 72.4 %all-gather.7.cloned.1.call-start = ((), (), s32[]{:S(2)}) async-start(), calls=%async_computation.5 | async-start | bytes 4055040 | tf_op jit(solution)/shard_map/all_gather | solution.py:85
  7.9 142.6 %all-gather.5.cloned.1.call-start = ((), (), s32[]{:S(2)}) async-start(), calls=%async_computation.3 | async-start | bytes 4055040 | tf_op jit(solution)/shard_map/all_gather | solution.py:86
  8.6 257.9 %reduce-scatter.6.cloned.1.call-start = ((), (), s32[]{:S(2)}) async-start(), calls=%async_computation.6 | async-start | bytes 8847360 | tf_op jit(solution)/shard_map/reduce_scatter | solution.py:100
  79.6 3.6 copy-start.1
  147.6 0.9 copy-start
  147.6 2.2 copy-start.6
  147.7 237.7 %reduce-scatter.4.cloned.1.call-start = ((), (), s32[]{:S(2)}) async-start(), calls=%async_computation.4 | async-start | bytes 8847360 | tf_op jit(solution)/shard_map/reduce_scatter | solution.py:101
  218.5 242.0 %all-gather.9.cloned.1.call-start = ((), (), s32[]{:S(2)}) async-start(), calls=%async_computation.7 | async-start | bytes 4423680 | tf_op jit(solution)/shard_map/all_gather | solution.py:107
  388.5 204.2 %all-gather.11.cloned.1.call-start = ((), (), s32[]{:S(2)}) async-start(), calls=%async_computation.9 | async-start | bytes 4423680 | tf_op jit(solution)/shard_map/all_gather | solution.py:106
  432.4 241.0 %reduce-scatter.8.cloned.1.call-start = ((), (), s32[]{:S(2)}) async-start(), calls=%async_computation.8 | async-start | bytes 8110080 | tf_op jit(solution)/shard_map/reduce_scatter | solution.py:115
  543.7 0.7 copy-start.4
  543.7 0.7 copy-start.5
  607.7 5.8 copy-start.2
  607.7 5.8 copy-start.3
  613.5 45.7 %copy-start.7 = (f32[30]{0:T(128)S(1)}, f32[30]{0:T(128)}, u32[]{:S(2)}) copy-start(f32[30]{0:T(128)} %compare_convert_fusion) | copy-start | bytes 364
Sparse Core Ops, SparseCore 0:
  9.9 69.6 all-gather.6
  81.4 66.2 all-gather.4
  151.9 114.5 reduce-scatter.5
  270.6 114.7 reduce-scatter.3
  388.6 71.8 all-gather.8
  463.5 72.1 all-gather.10
  543.9 129.4 reduce-scatter.7
where the time goes:
time: 692 us; the launch traced here: 682 us
  waiting for transfers between devices  266 us (38%)
  local copies, waits for them, and re-layouts  230 us (33%)
  matrix products  136 us (20%)
  other arithmetic  22.4 us (3%)
  between operations  15.7 us (2%)
  starting transfers between devices  9.35 us (1%)
    reduce_scatter x1, waiting for transfers between devices, body(): lax.psum_scatter(hidden_part, 'row', scatter_dimension=0, tiled=True)  119 us
    dot_general x18, matrix products, tile_term(): jnp.einsum('tsn,sf->tfn', products, placement, precision=lax.Precision.HI...  68.9 us
    all_gather x1, waiting for transfers between devices, body(): tokens_all = lax.all_gather(tokens, 'col', axis=0, tiled=True)  67.2 us
    reduce_scatter x1, waiting for transfers between devices, body(): lax.psum_scatter(pre_part, 'row', scatter_dimension=0, tiled=True)  47.9 us
    dot_general x12, matrix products, add_block(): jnp.einsum('tsk,tsn->skn', left_sel, right_sel, preferred_element_type=jn...  41.8 us
    dynamic_update_slice x36, local copies, waits for them, and re-layouts, by_blocks(): result = lax.map(function, stacked)  28.3 us
    unnamed x21, local copies, waits for them, and re-layouts  25.8 us
    dot_general x18, matrix products, tile_term(): jnp.einsum(einsum_form, chosen, blocks, preferred_element_type=jnp.float32)  25.6 us
  transfers between devices with their start and end apart: 7, of which 5 were waited for; matrix products, arithmetic and copies ran while one was open for 56% of the time, Pallas kernels for 0%

commit v1 on v0

v1 whole, which is shorter than its diff:
```python
import jax
import jax.numpy as jnp
from jax import lax
from jax.experimental import pallas as pl
from jax.experimental.pallas import tpu as pltpu
from jax.sharding import PartitionSpec as P

BLOCK = 64
CAP = 30
PAIRS = CAP // 2
NB = 10
ROWS = PAIRS * BLOCK
EXTRA = 16
TOK = 96
FEAT = NB * BLOCK
GROUP = 4 * TOK
SHIFT = 1024
SLAB = 5 * FEAT
MESH = pl.DeviceIdType.MESH
BF16 = jnp.bfloat16
F32 = jnp.float32

GELU_C = 0.7978845608028654
GELU_A = 0.044715


class Place:
    def __init__(self):
        self.p = lax.axis_index("row")
        col = lax.axis_index("col")
        self.z, self.xl, self.core = col // 4, (col // 2) % 2, col % 2
        self.y, self.xh = self.p // 2, self.p % 2
        self.f = (self.z + 7) % 8

    def col(self, z, xl, core):
        return z * 4 + xl * 2 + core

    def sibling(self):
        return (self.p, self.col(self.z, self.xl, 1 - self.core))

    def partner_lo(self):
        return (self.p, self.col(self.z, 1 - self.xl, self.core))

    def partner_hi(self):
        return (self.y * 2 + 1 - self.xh, self.col(self.z, self.xl, self.core))

    def along_y(self, step):
        return (((self.y + step + 4) % 4) * 2 + self.xh, self.col(self.z, self.xl, self.core))

    def along_z(self, step):
        return (self.p, self.col((self.z + step + 8) % 8, self.xl, self.core))

    def out_to(self):
        return ((self.z + 4 * self.core) % 8, self.col((self.p + 1) % 8, self.xl, self.core))

    def back_to(self):
        return (self.f, self.col((self.p + 8 - 4 * self.core) % 8, self.xl, self.core))

    def feature(self, step):
        return (self.z + step + 7 + 8) % 8


class Copies:
    def __init__(self, send_sems, recv_sems):
        self.send_sems, self.recv_sems = send_sems, recv_sems
        self.number = 0
        self.started = []

    def start(self, src, dst, device):
        copy = pltpu.make_async_remote_copy(
            src_ref=src,
            dst_ref=dst,
            send_sem=self.send_sems.at[self.number],
            recv_sem=self.recv_sems.at[self.number],
            device_id=device,
            device_id_type=MESH,
        )
        self.number += 1
        copy.start()
        self.started.append(copy)
        return copy

    def finish(self):
        for copy in self.started:
            copy.wait_send()


def greet(place):
    devices = [
        place.sibling(),
        place.partner_lo(),
        place.partner_hi(),
        place.along_y(1),
        place.along_y(-1),
        place.along_z(1),
        place.along_z(-1),
        place.out_to(),
        place.back_to(),
    ]
    barrier = pltpu.get_barrier_semaphore()
    for device in devices:
        pl.semaphore_signal(barrier, inc=1, device_id=device, device_id_type=MESH)
    pl.semaphore_wait(barrier, len(devices))


def gather_kernel(tok, out, pay, held, strip, own_sem, send_sems, recv_sems):
    place = Place()
    z, y, xh, xl, core = place.z, place.y, place.xh, place.xl, place.core
    greet(place)
    copies = Copies(send_sems, recv_sems)
    go = copies.start

    perm_tok = go(tok, held.at[0, place.p, core, xl], place.out_to())
    perm_out = go(out, held.at[1, place.p, core, xl], place.out_to())
    swap = go(pay, strip.at[:, y, xh], place.partner_hi())
    own = pltpu.make_async_copy(pay, strip.at[:, y, xh], own_sem)
    own.start()

    def toks(step):
        return held.at[0, place.feature(step), core]

    def outs(step):
        return held.at[1, place.feature(step), core, xl]

    def both_outs(step):
        return held.at[1, place.feature(step), core]

    def to_core(ref):
        return go(ref, ref, place.sibling())

    lo_outs, core_toks, core_outs = {}, [], []

    perm_tok.wait_recv()
    mine = held.at[0, place.f, core, xl]
    lo_tok = go(mine, mine, place.partner_lo())
    perm_out.wait_recv()
    right_out = go(outs(0), outs(0), place.along_z(1))
    left_out = go(outs(0), outs(0), place.along_z(-1))
    lo_outs[0] = go(outs(0), outs(0), place.partner_lo())
    lo_tok.wait_recv()
    right_tok = go(toks(0), toks(0), place.along_z(1))
    left_tok = go(toks(0), toks(0), place.along_z(-1))
    core_toks.append(to_core(toks(0)))

    swap.wait_recv()
    own.wait()
    ys = []
    for w in range(2):
        bundle = strip.at[w, y]
        ys.append((go(bundle, bundle, place.along_y(1)), go(bundle, bundle, place.along_y(-1))))

    for step in (1, 2, 3, 4):
        if step < 4:
            right_out.wait_recv()
            ref = outs(-step)
            if step < 3:
                right_out = go(ref, ref, place.along_z(1))
            lo_outs[-step] = go(ref, ref, place.partner_lo())
        left_out.wait_recv()
        ref = outs(step)
        if step < 4:
            left_out = go(ref, ref, place.along_z(-1))
        lo_outs[step] = go(ref, ref, place.partner_lo())

        right_tok.wait_recv()
        ref = toks(-step)
        if step < 4:
            right_tok = go(ref, ref, place.along_z(1))
        core_toks.append(to_core(ref))
        if step < 4:
            left_tok.wait_recv()
            ref = toks(step)
            if step < 3:
                left_tok = go(ref, ref, place.along_z(-1))
            core_toks.append(to_core(ref))

        if step == 1:
            up_far = strip.at[0, (y + 3) % 4]
            down_far = strip.at[1, (y + 1) % 4]
            ys[0][0].wait_recv()
            far_up = go(up_far, up_far, place.along_y(1))
            ys[1][1].wait_recv()
            far_down = go(down_far, down_far, place.along_y(-1))
        for done in ((0,), (-1, 1), (-2, 2), (-3, 3))[step - 1]:
            lo_outs[done].wait_recv()
            core_outs.append(to_core(both_outs(done)))
    lo_outs[4].wait_recv()
    core_outs.append(to_core(both_outs(4)))
    ys[0][1].wait_recv()
    ys[1][0].wait_recv()
    far_up.wait_recv()
    far_down.wait_recv()
    for copy in core_toks + core_outs:
        copy.wait_recv()
    copies.finish()


GATHER_COPIES = 3 + 1 + 2 * 7 + 8 + 16 + 6


def compute_kernel(place_ref, take_ref, held, strip, tok_part, up_part, down_part, up_dense, down_dense, blocks, pre, slope_part, hidden, pre_grad, grads):
    zeros = jnp.zeros((BLOCK, 128), BF16)
    blocks[ROWS : ROWS + BLOCK, :] = zeros
    blocks[SHIFT + ROWS : SHIFT + ROWS + BLOCK, :] = zeros

    def load_blocks(which, tile):
        data = strip[which, tile, 0:ROWS, :]
        blocks[0:ROWS, :] = data
        blocks[SHIFT : SHIFT + ROWS, :] = jnp.concatenate([data[:, BLOCK:], data[:, :BLOCK]], axis=1)

    def one_tile(tile, carry):
        load_blocks(0, tile)
        for i in range(NB):
            for j in range(NB):
                start = pl.multiple_of(place_ref[tile, i * NB + j], BLOCK)
                half = (j % 2) * BLOCK
                up_dense[tile, i * BLOCK : (i + 1) * BLOCK, j * BLOCK : (j + 1) * BLOCK] = blocks[
                    pl.ds(start, BLOCK), half : half + BLOCK
                ]
        load_blocks(1, tile)
        for i in range(NB):
            for j in range(NB):
                start = pl.multiple_of(place_ref[8 + tile, i * NB + j], BLOCK)
                half = (i % 2) * BLOCK
                down_dense[j * BLOCK : (j + 1) * BLOCK, i * BLOCK : (i + 1) * BLOCK] = blocks[
                    pl.ds(start, BLOCK), half : half + BLOCK
                ]
        pre[...] += jnp.dot(held[0, tile], up_dense[tile], preferred_element_type=F32)
        slope_part[...] += lax.dot_general(
            held[1, tile], down_dense[...], (((1,), (1,)), ((), ())), preferred_element_type=F32
        )
        return carry

    pre[...] = jnp.zeros_like(pre)
    slope_part[...] = jnp.zeros_like(slope_part)
    lax.fori_loop(0, 8, one_tile, 0)

    def activate(index, carry):
        rows = pl.ds(pl.multiple_of(index * 32, 32), 32)
        v = pre[rows, :]
        t = jnp.tanh(GELU_C * (v + GELU_A * v * v * v))
        hidden[rows, :] = (0.5 * v * (1.0 + t)).astype(BF16)
        slope = 0.5 * (1.0 + t) + 0.5 * v * (1.0 - t * t) * GELU_C * (1.0 + 3.0 * GELU_A * v * v)
        pre_grad[rows, :] = (slope_part[rows, :] * slope).astype(BF16)
        return carry

    lax.fori_loop(0, GROUP // 32, activate, 0)

    def extract(product, row, target, tile):
        product = product.astype(BF16)
        for slab in range(5):
            data = product[:, slab * 128 : (slab + 1) * 128]
            grads[slab * FEAT : (slab + 1) * FEAT, :] = data
            grads[SLAB + slab * FEAT : SLAB + (slab + 1) * FEAT, :] = jnp.concatenate(
                [data[:, BLOCK:], data[:, :BLOCK]], axis=1
            )
        for slot in range(CAP):
            start = pl.multiple_of(take_ref[row, slot], BLOCK)
            half = (slot % 2) * BLOCK
            place = (slot // 2) * BLOCK
            target[tile, place : place + BLOCK, half : half + BLOCK] = grads[pl.ds(start, BLOCK), half : half + BLOCK]

    def grad_tile(tile, carry):
        tok_part[tile] = lax.dot_general(
            pre_grad[...], up_dense[tile], (((1,), (1,)), ((), ())), preferred_element_type=F32
        ).astype(BF16)
        extract(
            lax.dot_general(held[0, tile], pre_grad[...], (((0,), (0,)), ((), ())), preferred_element_type=F32),
            tile, up_part, tile,
        )
        extract(
            lax.dot_general(hidden[...], held[1, tile], (((0,), (0,)), ((), ())), preferred_element_type=F32),
            8 + tile, down_part, tile,
        )
        return carry

    lax.fori_loop(0, 8, grad_tile, 0)


def add(*parts):
    total = parts[0].astype(F32)
    for part in parts[1:]:
        total = total + part.astype(F32)
    return total


def scatter_kernel(
    tok_part, up_part, down_part, tok_out, up_out, down_out,
    from_core, summed, right_in, left_in, right_far, left_far, lo_out, lo_in, home,
    y_far, y_right, y_left, y_send, hi_out, hi_in, send_sems, recv_sems,
):
    place = Place()
    y, xh, xl, core = place.y, place.xh, place.xl, place.core
    greet(place)
    copies = Copies(send_sems, recv_sems)
    go = copies.start

    core_in = {}
    for step in (4, 3, -3, 2, -2, 1, -1, 0):
        f = place.feature(step)
        core_in[step] = go(tok_part.at[f, 1 - core], from_core.at[f], place.sibling())

    far_up = go(up_part.at[(y + 2) % 4], y_far.at[0], place.along_y(1))
    far_down = go(down_part.at[(y + 2) % 4], y_far.at[1], place.along_y(-1))
    up_left = go(up_part.at[(y + 3) % 4], y_left.at[0], place.along_y(-1))
    down_right = go(down_part.at[(y + 1) % 4], y_right.at[1], place.along_y(1))

    def sum_core(step):
        f = place.feature(step)
        core_in[step].wait_recv()
        for half in range(2):
            summed[f, half] = add(tok_part[f, core, half], from_core[f, half]).astype(BF16)
        return f

    f = sum_core(4)
    go_right = go(summed.at[f, 0], right_far, place.along_z(1))
    go_left = go(summed.at[f, 1], left_far, place.along_z(-1))
    for step in (3, 2, 1):
        f = sum_core(step)
        go_right.wait_recv()
        if step == 3:
            summed[f, 0] = add(summed[f, 0], right_far[...]).astype(BF16)
        else:
            for half in range(2):
                summed[f, half] = add(summed[f, half], right_in[3 - step - 1, half]).astype(BF16)
        go_right = go(summed.at[f], right_in.at[3 - step], place.along_z(1))
        f = sum_core(-step)
        go_left.wait_recv()
        if step == 3:
            summed[f, 1] = add(summed[f, 1], left_far[...]).astype(BF16)
        else:
            for half in range(2):
                summed[f, half] = add(summed[f, half], left_in[3 - step - 1, half]).astype(BF16)
        go_left = go(summed.at[f], left_in.at[3 - step], place.along_z(-1))
        if step == 3:
            far_up.wait_recv()
            for side in range(2):
                y_send[0, side] = add(up_part[(y + 1) % 4, side], y_far[0, side]).astype(BF16)
            up_right = go(y_send.at[0], y_right.at[0], place.along_y(1))
            far_down.wait_recv()
            for side in range(2):
                y_send[1, side] = add(down_part[(y + 3) % 4, side], y_far[1, side]).astype(BF16)
            down_left = go(y_send.at[1], y_left.at[1], place.along_y(-1))

    f = sum_core(0)
    go_right.wait_recv()
    go_left.wait_recv()
    other = 1 - xl
    lo_out[...] = add(
        tok_part[f, core, other], from_core[f, other], right_in[2, other], left_in[2, other]
    ).astype(BF16)
    lo = go(lo_out, lo_in, place.partner_lo())

    up_left.wait_recv()
    up_right.wait_recv()
    down_left.wait_recv()
    down_right.wait_recv()
    far = 1 - xh
    hi_out[0] = add(up_part[y, far], y_left[0, far], y_right[0, far]).astype(BF16)
    hi_out[1] = add(down_part[y, far], y_left[1, far], y_right[1, far]).astype(BF16)
    hi = go(hi_out, hi_in, place.partner_hi())

    lo.wait_recv()
    home[...] = add(
        tok_part[f, core, xl], from_core[f, xl], right_in[2, xl], left_in[2, xl], lo_in[...]
    ).astype(BF16)
    back = go(home, tok_out, place.back_to())

    hi.wait_recv()
    up_out[...] = add(up_part[y, xh], y_left[0, xh], y_right[0, xh], hi_in[0])
    down_out[...] = add(down_part[y, xh], y_left[1, xh], y_right[1, xh], hi_in[1])
    back.wait_recv()
    copies.finish()


SCATTER_COPIES = 8 + 4 + 8 + 2 + 3


def vmem(count):
    return [pl.BlockSpec(memory_space=pltpu.VMEM)] * count


def hbm(count):
    return [pl.BlockSpec(memory_space=pl.ANY)] * count


def sds(shape, dtype=BF16):
    return jax.ShapeDtypeStruct(shape, dtype)


def payload(blocks, layout, counts):
    pairs = blocks[0, 0].reshape(PAIRS, 2, BLOCK, BLOCK).transpose(0, 2, 1, 3).reshape(ROWS, 2 * BLOCK)
    ids = layout[0, 0]
    slots = jnp.arange(CAP, dtype=jnp.int32)
    hit = (ids[:, None] == jnp.arange(128, dtype=jnp.int32)[None, :]) & (slots < counts[0, 0])[:, None]
    slot_of = CAP + jnp.sum(jnp.where(hit, slots[:, None] - CAP, 0), axis=0)
    extra = jnp.zeros((EXTRA, 128), jnp.int32).at[0].set(slot_of).at[1, :CAP].set(ids)
    return jnp.concatenate([pairs, extra.astype(BF16)], axis=0)


def offsets(extra):
    numbers = jnp.arange(128, dtype=jnp.int32)
    slot_of, ids = extra[:, :, 0].astype(jnp.int32), extra[:, :, 1].astype(jnp.int32)
    odd = jnp.stack([numbers % NB % 2, numbers // NB % 2])[:, None, :]
    place = ((slot_of % 2 + odd) % 2) * SHIFT + (slot_of // 2) * BLOCK
    i, j = ids // NB, ids % NB
    lane = jnp.stack([j[0], i[1]])
    row = jnp.stack([i[0], j[1]])
    take = ((lane % 2 + numbers % 2) % 2) * SLAB + (lane // 2) * FEAT + row * BLOCK
    return place.reshape(16, 128), take.reshape(16, 128)


def body(tokens, up_blocks, up_layout, up_counts, down_blocks, down_layout, down_counts, grad_out):
    pay = jnp.stack([payload(up_blocks, up_layout, up_counts), payload(down_blocks, down_layout, down_counts)])
    held, strip = pl.pallas_call(
        gather_kernel,
        out_shape=(sds((2, 8, 2, 2, TOK, FEAT)), sds((2, 4, 2, ROWS + EXTRA, 128))),
        in_specs=hbm(3),
        out_specs=tuple(hbm(2)),
        scratch_shapes=[
            pltpu.SemaphoreType.DMA,
            pltpu.SemaphoreType.DMA((GATHER_COPIES,)),
            pltpu.SemaphoreType.DMA((GATHER_COPIES,)),
        ],
        compiler_params=pltpu.CompilerParams(collective_id=0, has_side_effects=True),
        name="gather",
    )(tokens, grad_out, pay)
    held = held.reshape(2, 8, GROUP, FEAT)
    strip = strip.reshape(2, 8, ROWS + EXTRA, 128)
    place, take = offsets(strip[:, :, ROWS : ROWS + 2])
    tok_part, up_part, down_part = pl.pallas_call(
        compute_kernel,
        out_shape=(sds((8, GROUP, FEAT)), sds((8, ROWS, 128)), sds((8, ROWS, 128))),
        in_specs=[pl.BlockSpec(memory_space=pltpu.SMEM)] * 2 + vmem(2),
        out_specs=tuple(vmem(3)),
        scratch_shapes=[
            pltpu.VMEM((8, FEAT, FEAT), BF16),
            pltpu.VMEM((FEAT, FEAT), BF16),
            pltpu.VMEM((2 * SHIFT, 128), BF16),
            pltpu.VMEM((GROUP, FEAT), F32),
            pltpu.VMEM((GROUP, FEAT), F32),
            pltpu.VMEM((GROUP, FEAT), BF16),
            pltpu.VMEM((GROUP, FEAT), BF16),
            pltpu.VMEM((2 * SLAB, 128), BF16),
        ],
        compiler_params=pltpu.CompilerParams(vmem_limit_bytes=56 * 2**20),
        name="compute",
    )(place, take, held, strip)
    tok_grad, up_sum, down_sum = pl.pallas_call(
        scatter_kernel,
        out_shape=(sds((TOK, FEAT)), sds((ROWS, 128), F32), sds((ROWS, 128), F32)),
        in_specs=vmem(3),
        out_specs=tuple(vmem(3)),
        scratch_shapes=[
            pltpu.VMEM((8, 2, TOK, FEAT), BF16),
            pltpu.VMEM((8, 2, TOK, FEAT), BF16),
            pltpu.VMEM((3, 2, TOK, FEAT), BF16),
            pltpu.VMEM((3, 2, TOK, FEAT), BF16),
            pltpu.VMEM((TOK, FEAT), BF16),
            pltpu.VMEM((TOK, FEAT), BF16),
            pltpu.VMEM((TOK, FEAT), BF16),
            pltpu.VMEM((TOK, FEAT), BF16),
            pltpu.VMEM((TOK, FEAT), BF16),
            pltpu.VMEM((2, 2, ROWS, 128), BF16),
            pltpu.VMEM((2, 2, ROWS, 128), BF16),
            pltpu.VMEM((2, 2, ROWS, 128), BF16),
            pltpu.VMEM((2, 2, ROWS, 128), BF16),
            pltpu.VMEM((2, ROWS, 128), BF16),
            pltpu.VMEM((2, ROWS, 128), BF16),
            pltpu.SemaphoreType.DMA((SCATTER_COPIES,)),
            pltpu.SemaphoreType.DMA((SCATTER_COPIES,)),
        ],
        compiler_params=pltpu.CompilerParams(collective_id=1, has_side_effects=True, vmem_limit_bytes=48 * 2**20),
        name="scatter",
    )(
        tok_part.reshape(8, 2, 2, TOK, FEAT),
        up_part.reshape(4, 2, ROWS, 128),
        down_part.reshape(4, 2, ROWS, 128),
    )

    def slots(total, counts):
        flat = total.reshape(PAIRS, BLOCK, 2, BLOCK).transpose(0, 2, 1, 3).reshape(CAP, BLOCK * BLOCK)
        live = jnp.arange(CAP, dtype=jnp.int32) < counts[0, 0]
        return jnp.where(live[:, None], flat, 0.0)[None, None]

    return tok_grad, slots(up_sum, up_counts), slots(down_sum, down_counts)


def solution(mesh):
    in_specs = (
        P("col", "row"),
        P("row", "col", None, None),
        P("row", "col", None),
        P("row", "col"),
        P("row", "col", None, None),
        P("row", "col", None),
        P("row", "col"),
        P("col", "row"),
    )
    out_specs = (P("col", "row"), P("row", "col", None, None), P("row", "col", None, None))
    return jax.shard_map(body, mesh=mesh, in_specs=in_specs, out_specs=out_specs, check_vma=False)
```

time: 692 us -> 203 us (0.29)
  the two profiles are of different devices: /device:TPU:24 before, /device:TPU:48 now
where the time goes in v1:
time: 203 us; the launch traced here: 199 us
  Pallas kernels  177 us (87%)
  local copies, waits for them, and re-layouts  12.3 us (6%)
  other arithmetic  7.95 us (4%)
  between operations  2.15 us (1%)
    pallas_call x1, Pallas kernels, body(): pl.pallas_call(gather_kernel, out_shape=(sds((2, 8, 2, 2, TOK, FEAT)), sd...  87.2 us
    pallas_call x1, Pallas kernels, body(): pl.pallas_call(scatter_kernel, out_shape=(sds((TOK, FEAT)), sds((ROWS, 12...  54.3 us
    pallas_call x1, Pallas kernels, body(): pl.pallas_call(compute_kernel, out_shape=(sds((8, GROUP, FEAT)), sds((8,...  35.4 us

profile of v1, /device:TPU:48, one launch (start us, length us, event | category | flops | bytes accessed | tf_op | source)
XLA Modules:
  0.0 199.4 jit_solution(15588467568412117081)
XLA Ops:
  2.0 0.8 select_reduce_fusion.1
  2.8 0.8 scatter.24
  3.6 0.8 scatter.16
  4.4 1.4 reshape_squeeze.6
  5.9 0.5 copy.35
  6.4 0.2 reshape.370
  6.6 1.4 reshape_squeeze.7
  8.1 0.5 copy.34
  8.6 0.2 reshape.372
  8.9 0.8 pad_maximum_fusion.pay
  9.7 87.2 %gather.1 = (bf16[2,8,2,2,96,640]{5,4,3,2,1,0:T(8,128)(2,1)}, bf16[2,4,2,976,128]{4,3,2,1,0:T(8,128)(2,1)}) custom-call(bf16[96,640]{1,0:T(8,128)(2,1)} %tok.1, bf16[96,640]{1,0:T(8,128)(2,1)} %out.1, bf16[2,976,128]{2,1,0:T(8,128)(2,1)} %pad_maximum_fusion.pay), custom_call_target="tpu_custom_call" | custom-call | tf_op jit(solution)/shard_map/gather/pallas_call | solution.py:415
  96.9 1.4 fusion.23
  98.3 0.9 slice_convert_fusion
  99.2 0.6 fusion.5.place_ref
  99.8 0.6 fusion.11.take_ref
  100.5 35.4 %compute.1 = (bf16[8,384,640]{2,1,0:T(8,128)(2,1)}, bf16[8,960,128]{2,1,0:T(8,128)(2,1)}, bf16[8,960,128]{2,1,0:T(8,128)(2,1)}) custom-call(s32[16,128]{1,0:T(8,128)} %fusion.5.place_ref, s32[16,128]{1,0:T(8,128)} %fusion.11.take_ref, bf16[2,8,384,640]{3,2,1,0:T(8,128)(2,1)} %bitcast.69, bf16[2,8,976,128]{3,2,1,0:T(8,128)(2,1)} %bitcast.72), custom_call_target="tpu_custom_call" | custom-call | tf_op jit(solution)/shard_map/compute/pallas_call | solution.py:431
  135.9 0.0 copy-start
  135.9 1.5 copy-done
  137.5 0.0 copy-start.1
  137.5 1.5 copy-done.1
  139.0 54.3 %scatter.25 = (bf16[96,640]{1,0:T(8,128)(2,1)S(1)}, f32[960,128]{1,0:T(8,128)S(1)}, f32[960,128]{1,0:T(8,128)S(1)}) custom-call(bf16[8,2,2,96,640]{4,3,2,1,0:T(8,128)(2,1)} %bitcast.73, bf16[4,2,960,128]{3,2,1,0:T(8,128)(2,1)S(1)} %bitcast.67, bf16[4,2,960,128]{3,2,1,0:T(8,128)(2,1)S(1)} %bitcast.68), custom_call_target="tpu_custom_call" | custom-call | tf_op jit(solution)/shard_map/scatter/pallas_call | solution.py:449
  193.3 0.6 reshape.379
  193.9 0.1 copy.30
  194.0 0.6 reshape.380
  194.7 1.3 broadcast_select_fusion.1
  196.0 0.6 reshape.381
  196.6 0.1 copy.31
  196.7 0.6 reshape.382
  197.4 1.3 broadcast_select_fusion
  198.7 0.6 copy.41
  (17 shorter events, 0.1 us)
Async XLA Ops:
  135.9 1.5 copy-start
  137.5 1.5 copy-start.1

commit v2 on v1

v2 whole, which is shorter than its diff:
```python
import jax
import jax.numpy as jnp
from jax import lax
from jax.experimental import pallas as pl
from jax.experimental.pallas import tpu as pltpu
from jax.sharding import PartitionSpec as P

BLOCK = 64
CAP = 30
PAIRS = CAP // 2
NB = 10
ROWS = PAIRS * BLOCK
EXTRA = 16
TOK = 96
FEAT = NB * BLOCK
GROUP = 4 * TOK
SHIFT = 16
SLAB = 5 * NB
MESH = pl.DeviceIdType.MESH
BF16 = jnp.bfloat16
F32 = jnp.float32

GELU_C = 0.7978845608028654
GELU_A = 0.044715


class Place:
    def __init__(self):
        self.p = lax.axis_index("row")
        col = lax.axis_index("col")
        self.z, self.xl, self.core = col // 4, (col // 2) % 2, col % 2
        self.y, self.xh = self.p // 2, self.p % 2
        self.f = (self.z + 7) % 8

    def col(self, z, xl, core):
        return z * 4 + xl * 2 + core

    def sibling(self):
        return (self.p, self.col(self.z, self.xl, 1 - self.core))

    def partner_lo(self):
        return (self.p, self.col(self.z, 1 - self.xl, self.core))

    def partner_hi(self):
        return (self.y * 2 + 1 - self.xh, self.col(self.z, self.xl, self.core))

    def along_y(self, step):
        return (((self.y + step + 4) % 4) * 2 + self.xh, self.col(self.z, self.xl, self.core))

    def along_z(self, step):
        return (self.p, self.col((self.z + step + 8) % 8, self.xl, self.core))

    def out_to(self):
        return ((self.z + 4 * self.core) % 8, self.col((self.p + 1) % 8, self.xl, self.core))

    def back_to(self):
        return (self.f, self.col((self.p + 8 - 4 * self.core) % 8, self.xl, self.core))

    def feature(self, step):
        return (self.z + step + 7 + 8) % 8


class Copies:
    def __init__(self, send_sems, recv_sems):
        self.send_sems, self.recv_sems = send_sems, recv_sems
        self.number = 0
        self.made = []

    def reserve(self, count):
        first = self.number
        self.number += count
        return first

    def copy(self, src, dst, device, index):
        return pltpu.make_async_remote_copy(
            src_ref=src,
            dst_ref=dst,
            send_sem=self.send_sems.at[index],
            recv_sem=self.recv_sems.at[index],
            device_id=device,
            device_id_type=MESH,
        )

    def start(self, src, dst, device):
        copy = self.copy(src, dst, device, self.reserve(1))
        copy.start()
        self.made.append(copy)
        return copy

    def started(self, src, dst, device, index):
        copy = self.copy(src, dst, device, index)
        self.made.append(copy)
        return copy

    def finish(self):
        for copy in self.made:
            copy.wait_send()


def greet(place):
    devices = [
        place.sibling(),
        place.partner_lo(),
        place.partner_hi(),
        place.along_y(1),
        place.along_y(-1),
        place.along_z(1),
        place.along_z(-1),
        place.out_to(),
        place.back_to(),
    ]
    barrier = pltpu.get_barrier_semaphore()
    for device in devices:
        pl.semaphore_signal(barrier, inc=1, device_id=device, device_id_type=MESH)
    pl.semaphore_wait(barrier, len(devices))


def add(*parts):
    total = parts[0].astype(F32)
    for part in parts[1:]:
        total = total + part.astype(F32)
    return total


def kernel(
    tok, out, pay, meta,
    tok_out, up_out, down_out,
    held, strip, numbers, numbers_sm, dense, blocks, pre, slope_part, hidden, pre_grad, grads,
    own_tok, core_send, from_core, tok_send, right_in, left_in, right_far, left_far, lo_out, lo_in, home,
    part, y_far, y_right, y_left, y_send, hi_out, hi_in,
    meta_sems, send_sems, recv_sems,
):
    place = Place()
    z, y, xh, xl, core = place.z, place.y, place.xh, place.xl, place.core
    mine, twin = place.p, y * 2 + 1 - xh
    right, left = place.along_y(1), place.along_y(-1)
    greet(place)
    copies = Copies(send_sems, recv_sems)
    go = copies.start

    perm_tok = go(tok, held.at[0, place.p, core, xl], place.out_to())
    perm_out = go(out, held.at[1, place.p, core, xl], place.out_to())
    swap_meta = go(meta, numbers.at[mine], place.partner_hi())
    swap = go(pay, strip.at[:, mine], place.partner_hi())

    def to_scalars(source, tile, index):
        copy = pltpu.make_async_copy(source, numbers_sm.at[tile], meta_sems.at[index])
        copy.start()
        return copy

    def fill(which, tile, data):
        turned = jnp.concatenate([data[:, BLOCK:], data[:, :BLOCK]], axis=1)
        blocks[0:PAIRS] = data.reshape(PAIRS, BLOCK, 128)
        blocks[SHIFT : SHIFT + PAIRS] = turned.reshape(PAIRS, BLOCK, 128)
        for i in range(NB):
            for j in range(NB):
                half = (j % 2) * BLOCK
                dense[which, tile, i * BLOCK : (i + 1) * BLOCK, j * BLOCK : (j + 1) * BLOCK] = blocks[
                    numbers_sm[tile, which, i * NB + j], :, half : half + BLOCK
                ]

    def fill_tiles(tiles):
        def step(index, carry):
            which, tile = index % 2, tiles(index // 2)
            fill(which, tile, strip[which, tile])
            return carry

        return step

    zeros = jnp.zeros((BLOCK, 128), BF16)
    blocks[PAIRS] = zeros
    blocks[SHIFT + PAIRS] = zeros
    pre[...] = jnp.zeros_like(pre)
    slope_part[...] = jnp.zeros_like(slope_part)
    to_scalars(meta, mine, 0).wait()

    def fill_mine(which, carry):
        fill(which, mine, pay[which])
        return carry

    lax.fori_loop(0, 2, fill_mine, 0)

    def toks(step):
        return held.at[0, place.feature(step), core]

    def outs(step):
        return held.at[1, place.feature(step), core, xl]

    def both_outs(step):
        return held.at[1, place.feature(step), core]

    def to_core(ref):
        return go(ref, ref, place.sibling())

    lo_outs, core_toks, core_outs = {}, {}, {}

    perm_tok.wait_recv()
    piece = held.at[0, place.f, core, xl]
    lo_tok = go(piece, piece, place.partner_lo())
    meta_right = go(meta, numbers.at[mine], right)
    meta_left = go(meta, numbers.at[mine], left)
    near = [
        [go(pay.at[w], strip.at[w, mine], right), go(pay.at[w], strip.at[w, mine], left)] for w in range(2)
    ]

    lo_tok.wait_recv()
    right_tok = go(toks(0), toks(0), place.along_z(1))
    left_tok = go(toks(0), toks(0), place.along_z(-1))
    core_toks[0] = to_core(toks(0))

    swap_meta.wait_recv()
    ref = numbers.at[twin]
    twin_meta_right = go(ref, ref, right)
    twin_meta_left = go(ref, ref, left)
    twin_scalars = to_scalars(ref, twin, 1)
    swap.wait_recv()
    near_twin = []
    for w in range(2):
        ref = strip.at[w, twin]
        near_twin.append([go(ref, ref, right), go(ref, ref, left)])
    twin_scalars.wait()
    lax.fori_loop(0, 2, fill_tiles(lambda index: twin), 0)

    perm_out.wait_recv()
    right_out = go(outs(0), outs(0), place.along_z(1))
    left_out = go(outs(0), outs(0), place.along_z(-1))
    lo_outs[0] = go(outs(0), outs(0), place.partner_lo())

    def tile_at(step, side):
        return ((y + step + 4) % 4) * 2 + (xh + side) % 2

    def multiply(step):
        f = place.feature(step)
        t = held[0, f].reshape(GROUP, FEAT)
        pre[...] += jnp.dot(t, dense[0, f], preferred_element_type=F32)
        g = held[1, f].reshape(GROUP, FEAT)
        slope_part[...] += lax.dot_general(g, dense[1, f], (((1,), (1,)), ((), ())), preferred_element_type=F32)

    def multiply_ready(steps):
        for step in steps:
            core_toks[step].wait_recv()
            core_outs[step].wait_recv()

    far_copies = []
    for step in (1, 2, 3, 4):
        if step < 4:
            right_out.wait_recv()
            ref = outs(-step)
            if step < 3:
                right_out = go(ref, ref, place.along_z(1))
            lo_outs[-step] = go(ref, ref, place.partner_lo())
        left_out.wait_recv()
        ref = outs(step)
        if step < 4:
            left_out = go(ref, ref, place.along_z(-1))
        lo_outs[step] = go(ref, ref, place.partner_lo())

        right_tok.wait_recv()
        ref = toks(-step)
        if step < 4:
            right_tok = go(ref, ref, place.along_z(1))
        core_toks[-step] = to_core(ref)
        if step < 4:
            left_tok.wait_recv()
            ref = toks(step)
            if step < 3:
                left_tok = go(ref, ref, place.along_z(-1))
            core_toks[step] = to_core(ref)
        if step == 4:
            core_toks[4] = core_toks[-4]

        if step in (1, 2):
            side = step - 1
            came, met = (near, (meta_right, meta_left)) if side == 0 else (near_twin, (twin_meta_right, twin_meta_left))
            from_left, from_right = tile_at(-1, side), tile_at(1, side)
            met[0].wait_recv()
            far_meta = go(numbers.at[from_left], numbers.at[from_left], right)
            scalars = [to_scalars(numbers.at[from_left], from_left, 2 + 3 * side)]
            met[1].wait_recv()
            scalars.append(to_scalars(numbers.at[from_right], from_right, 3 + 3 * side))
            came[0][0].wait_recv()
            ref = strip.at[0, from_left]
            far_up = go(ref, ref, right)
            came[1][1].wait_recv()
            ref = strip.at[1, from_right]
            far_down = go(ref, ref, left)
            came[0][1].wait_recv()
            came[1][0].wait_recv()
            for copy in scalars:
                copy.wait()
            far_copies.append((far_meta, far_up, far_down))
            lax.fori_loop(0, 4, fill_tiles(lambda index, side=side: tile_at(2 * index - 1, side)), 0)
        for done in ((0,), (-1, 1), (-2, 2), (-3, 3))[step - 1]:
            lo_outs[done].wait_recv()
            core_outs[done] = to_core(both_outs(done))
        if step == 3:
            scalars = []
            for side in range(2):
                tile = tile_at(2, side)
                far_copies[side][0].wait_recv()
                scalars.append(to_scalars(numbers.at[tile], tile, 4 + 3 * side))
            for side in range(2):
                far_copies[side][1].wait_recv()
                far_copies[side][2].wait_recv()
            for copy in scalars:
                copy.wait()
            lax.fori_loop(0, 4, fill_tiles(lambda index: tile_at(2, index)), 0)
            multiply_ready((0, -1, 1))

            def near_features(index, carry):
                multiply(index - 1)
                return carry

            lax.fori_loop(0, 3, near_features, 0)
    lo_outs[4].wait_recv()
    core_outs[4] = to_core(both_outs(4))
    multiply_ready((-2, 2, -3, 3))

    def late_features(index, carry):
        multiply(2 + index + index // 2)
        return carry

    lax.fori_loop(0, 4, late_features, 0)
    multiply_ready((4,))
    multiply(4)

    def activate(index, carry):
        rows = pl.ds(pl.multiple_of(index * 32, 32), 32)
        v = pre[rows, :]
        t = jnp.tanh(GELU_C * (v + GELU_A * v * v * v))
        hidden[rows, :] = (0.5 * v * (1.0 + t)).astype(BF16)
        slope = 0.5 * (1.0 + t) + 0.5 * v * (1.0 - t * t) * GELU_C * (1.0 + 3.0 * GELU_A * v * v)
        pre_grad[rows, :] = (slope_part[rows, :] * slope).astype(BF16)
        return carry

    lax.fori_loop(0, GROUP // 32, activate, 0)

    def extract(product, which, tile):
        product = product.astype(BF16)
        for slab in range(5):
            data = product[:, slab * 128 : (slab + 1) * 128]
            turned = jnp.concatenate([data[:, BLOCK:], data[:, :BLOCK]], axis=1)
            grads[slab * NB : (slab + 1) * NB] = data.reshape(NB, BLOCK, 128)
            grads[SLAB + slab * NB : SLAB + (slab + 1) * NB] = turned.reshape(NB, BLOCK, 128)
        for slot in range(CAP):
            half = (slot % 2) * BLOCK
            at = (slot // 2) * BLOCK
            part[which, tile, at : at + BLOCK, half : half + BLOCK] = grads[
                numbers_sm[tile, 2 + which, slot], :, half : half + BLOCK
            ]

    def up_tile(tile):
        left_side = held[0, tile].reshape(GROUP, FEAT)
        extract(
            lax.dot_general(left_side, pre_grad[...], (((0,), (0,)), ((), ())), preferred_element_type=F32), 0, tile
        )

    def down_tile(tile):
        right_side = held[1, tile].reshape(GROUP, FEAT)
        extract(
            lax.dot_general(hidden[...], right_side, (((0,), (0,)), ((), ())), preferred_element_type=F32), 1, tile
        )

    half_rows = GROUP // 2

    def tok_feature(f, index):
        def rows_of(which_core):
            rows = pre_grad[pl.ds(pl.multiple_of(which_core * half_rows, half_rows), half_rows), :]
            return lax.dot_general(rows, dense[0, f], (((1,), (1,)), ((), ())), preferred_element_type=F32)

        core_send[f] = rows_of(1 - core).astype(BF16).reshape(2, TOK, FEAT)
        copies.copy(core_send.at[f], from_core.at[f], place.sibling(), index).start()
        own_tok[f] = rows_of(core).reshape(2, TOK, FEAT)

    core_first = copies.reserve(8)
    core_in = {}

    def tok_features(first, steps, step_of):
        def one(index, carry):
            tok_feature(place.feature(step_of(index)), core_first + first + index)
            return carry

        lax.fori_loop(0, len(steps), one, 0)
        for number, step in enumerate(steps):
            f = place.feature(step)
            core_in[step] = copies.started(
                core_send.at[f], from_core.at[f], place.sibling(), core_first + first + number
            )

    def far_tiles(index, carry):
        tile = tile_at(2, 1 - index)
        up_tile(tile)
        copies.copy(part.at[0, tile], y_far.at[0, 1 - index], right, far_first + index).start()
        down_tile(tile)
        copies.copy(part.at[1, tile], y_far.at[1, 1 - index], left, far_first + 2 + index).start()
        return carry

    far_first = copies.reserve(4)
    lax.fori_loop(0, 2, far_tiles, 0)
    far_in = [
        [copies.started(part.at[0, tile_at(2, side)], y_far.at[0, side], right, far_first + 1 - side) for side in range(2)],
        [copies.started(part.at[1, tile_at(2, side)], y_far.at[1, side], left, far_first + 3 - side) for side in range(2)],
    ]

    tok_features(0, (4, 3, -3), lambda index: 4 - index + (index // 2) * 3)

    def near_tiles(index, carry):
        tile = tile_at(1, 1 - index)
        down_tile(tile)
        copies.copy(part.at[1, tile], y_right.at[1, 1 - index], right, near_first + index).start()
        tile = tile_at(-1, 1 - index)
        up_tile(tile)
        copies.copy(part.at[0, tile], y_left.at[0, 1 - index], left, near_first + 2 + index).start()
        return carry

    near_first = copies.reserve(4)
    lax.fori_loop(0, 2, near_tiles, 0)
    down_right = [
        copies.started(part.at[1, tile_at(1, side)], y_right.at[1, side], right, near_first + 1 - side) for side in range(2)
    ]
    up_left = [
        copies.started(part.at[0, tile_at(-1, side)], y_left.at[0, side], left, near_first + 3 - side) for side in range(2)
    ]

    f = place.feature(4)
    core_in[4].wait_recv()
    tok_send[0] = add(own_tok[f], from_core[f]).astype(BF16)
    go_right = go(tok_send.at[0, 0], right_far, place.along_z(1))
    go_left = go(tok_send.at[0, 1], left_far, place.along_z(-1))

    tok_features(3, (2, -2), lambda index: 2 + 4 * index)

    def pass_on(step):
        nonlocal go_right, go_left
        f = place.feature(step)
        core_in[step].wait_recv()
        go_right.wait_recv()
        slot = 2 * (4 - step) - 1
        if step == 3:
            tok_send[slot, 0] = add(own_tok[f, 0], from_core[f, 0], right_far[...]).astype(BF16)
            tok_send[slot, 1] = add(own_tok[f, 1], from_core[f, 1]).astype(BF16)
        else:
            tok_send[slot] = add(own_tok[f], from_core[f], right_in[2 - step]).astype(BF16)
        go_right = go(tok_send.at[slot], right_in.at[3 - step], place.along_z(1))
        f = place.feature(-step)
        core_in[-step].wait_recv()
        go_left.wait_recv()
        if step == 3:
            tok_send[slot + 1, 0] = add(own_tok[f, 0], from_core[f, 0]).astype(BF16)
            tok_send[slot + 1, 1] = add(own_tok[f, 1], from_core[f, 1], left_far[...]).astype(BF16)
        else:
            tok_send[slot + 1] = add(own_tok[f], from_core[f], left_in[2 - step]).astype(BF16)
        go_left = go(tok_send.at[slot + 1], left_in.at[3 - step], place.along_z(-1))

    pass_on(3)

    def up_more(index, carry):
        up_tile(tile_at(1, 1 - index))
        down_tile(tile_at(-1, 1 - index))
        return carry

    lax.fori_loop(0, 2, up_more, 0)
    up_right, down_left = [None, None], [None, None]
    for side in (1, 0):
        far_in[0][side].wait_recv()
        y_send[0, side] = add(part[0, tile_at(1, side)], y_far[0, side]).astype(BF16)
        up_right[side] = go(y_send.at[0, side], y_right.at[0, side], right)
        far_in[1][side].wait_recv()
        y_send[1, side] = add(part[1, tile_at(-1, side)], y_far[1, side]).astype(BF16)
        down_left[side] = go(y_send.at[1, side], y_left.at[1, side], left)

    tok_features(5, (1, -1, 0), lambda index: 1 + 6 * index - (index // 2) * 5)
    pass_on(2)

    def own_tiles(index, carry):
        up_tile(tile_at(0, 1 - index))
        down_tile(tile_at(0, 1 - index))
        return carry

    lax.fori_loop(0, 2, own_tiles, 0)
    pass_on(1)

    hi = []
    up_left[1].wait_recv()
    up_right[1].wait_recv()
    hi_out[0] = add(part[0, twin], y_left[0, 1], y_right[0, 1]).astype(BF16)
    hi.append(go(hi_out.at[0], hi_in.at[0], place.partner_hi()))
    down_left[1].wait_recv()
    down_right[1].wait_recv()
    hi_out[1] = add(part[1, twin], y_left[1, 1], y_right[1, 1]).astype(BF16)
    hi.append(go(hi_out.at[1], hi_in.at[1], place.partner_hi()))

    f = place.f
    core_in[0].wait_recv()
    go_right.wait_recv()
    go_left.wait_recv()
    other = 1 - xl
    lo_out[...] = add(own_tok[f, other], from_core[f, other], right_in[2, other], left_in[2, other]).astype(BF16)
    lo = go(lo_out, lo_in, place.partner_lo())
    lo.wait_recv()
    home[...] = add(own_tok[f, xl], from_core[f, xl], right_in[2, xl], left_in[2, xl], lo_in[...]).astype(BF16)
    back = go(home, tok_out, place.back_to())

    for which, outputs, first, second in ((0, up_out, up_left, up_right), (1, down_out, down_left, down_right)):
        first[0].wait_recv()
        second[0].wait_recv()
        hi[which].wait_recv()
        outputs[...] = add(part[which, mine], y_left[which, 0], y_right[which, 0], hi_in[which])
    back.wait_recv()
    copies.finish()


COPIES = 93


def vmem(count):
    return [pl.BlockSpec(memory_space=pltpu.VMEM)] * count


def sds(shape, dtype=BF16):
    return jax.ShapeDtypeStruct(shape, dtype)


def offsets(up_layout, up_counts, down_layout, down_counts):
    up_ids, down_ids = up_layout[0, 0], down_layout[0, 0]
    ids = jnp.stack([up_ids, (down_ids % NB) * NB + down_ids // NB])
    counts = jnp.stack([up_counts[0, 0], down_counts[0, 0]])
    numbers = jnp.arange(128, dtype=jnp.int32)
    slots = numbers[:CAP]
    hit = (ids[:, :, None] == numbers) & (slots[None, :] < counts[:, None])[:, :, None]
    slot_of = CAP + jnp.sum(jnp.where(hit, slots[None, :, None] - CAP, 0), axis=1)
    place = ((slot_of + numbers % NB) % 2) * SHIFT + slot_of // 2
    row, lane = ids // NB, ids % NB
    take = ((lane + slots) % 2) * SLAB + (lane // 2) * NB + row
    take = jnp.pad(take, ((0, 0), (0, 128 - CAP)))
    return jnp.concatenate([place, take, jnp.zeros((4, 128), jnp.int32)], axis=0)


def body(tokens, up_blocks, up_layout, up_counts, down_blocks, down_layout, down_counts, grad_out):
    pay = jnp.stack([up_blocks[0, 0], down_blocks[0, 0]]).reshape(2, PAIRS, 2, BLOCK, BLOCK)
    pay = pay.transpose(0, 1, 3, 2, 4).reshape(2, ROWS, 2 * BLOCK)
    meta = offsets(up_layout, up_counts, down_layout, down_counts)
    tile = (ROWS, 128)
    piece = (TOK, FEAT)
    tok_grad, up_sum, down_sum = pl.pallas_call(
        kernel,
        out_shape=(sds(piece), sds(tile, F32), sds(tile, F32)),
        in_specs=vmem(4),
        out_specs=tuple(vmem(3)),
        scratch_shapes=[
            pltpu.VMEM((2, 8, 2, 2) + piece, BF16),
            pltpu.VMEM((2, 8) + tile, BF16),
            pltpu.VMEM((8, 8, 128), jnp.int32),
            pltpu.SMEM((8, 8, 128), jnp.int32),
            pltpu.VMEM((2, 8, FEAT, FEAT), BF16),
            pltpu.VMEM((2 * SHIFT, BLOCK, 128), BF16),
            pltpu.VMEM((GROUP, FEAT), F32),
            pltpu.VMEM((GROUP, FEAT), F32),
            pltpu.VMEM((GROUP, FEAT), BF16),
            pltpu.VMEM((GROUP, FEAT), BF16),
            pltpu.VMEM((2 * SLAB, BLOCK, 128), BF16),
            pltpu.VMEM((8, 2) + piece, F32),
            pltpu.VMEM((8, 2) + piece, BF16),
            pltpu.VMEM((8, 2) + piece, BF16),
            pltpu.VMEM((7, 2) + piece, BF16),
            pltpu.VMEM((3, 2) + piece, BF16),
            pltpu.VMEM((3, 2) + piece, BF16),
            pltpu.VMEM(piece, BF16),
            pltpu.VMEM(piece, BF16),
            pltpu.VMEM(piece, BF16),
            pltpu.VMEM(piece, BF16),
            pltpu.VMEM(piece, BF16),
            pltpu.VMEM((2, 8) + tile, BF16),
            pltpu.VMEM((2, 2) + tile, BF16),
            pltpu.VMEM((2, 2) + tile, BF16),
            pltpu.VMEM((2, 2) + tile, BF16),
            pltpu.VMEM((2, 2) + tile, BF16),
            pltpu.VMEM((2,) + tile, BF16),
            pltpu.VMEM((2,) + tile, BF16),
            pltpu.SemaphoreType.DMA((8,)),
            pltpu.SemaphoreType.DMA((COPIES,)),
            pltpu.SemaphoreType.DMA((COPIES,)),
        ],
        compiler_params=pltpu.CompilerParams(collective_id=0, has_side_effects=True, vmem_limit_bytes=60 * 2**20),
        name="layer",
    )(tokens, grad_out, pay, meta)

    def slots(total, counts):
        flat = total.reshape(PAIRS, BLOCK, 2, BLOCK).transpose(0, 2, 1, 3).reshape(CAP, BLOCK * BLOCK)
        live = jnp.arange(CAP, dtype=jnp.int32) < counts[0, 0]
        return jnp.where(live[:, None], flat, 0.0)[None, None]

    return tok_grad, slots(up_sum, up_counts), slots(down_sum, down_counts)


def solution(mesh):
    in_specs = (
        P("col", "row"),
        P("row", "col", None, None),
        P("row", "col", None),
        P("row", "col"),
        P("row", "col", None, None),
        P("row", "col", None),
        P("row", "col"),
        P("col", "row"),
    )
    out_specs = (P("col", "row"), P("row", "col", None, None), P("row", "col", None, None))
    return jax.shard_map(body, mesh=mesh, in_specs=in_specs, out_specs=out_specs, check_vma=False)
```

time: 203 us -> 161 us (0.79)
  the two profiles are of different devices: /device:TPU:48 before, /device:TPU:50 now
where the time goes in v2:
time: 161 us
  Pallas kernels  144 us (89%)
  local copies, waits for them, and re-layouts  10.8 us (7%)
  other arithmetic  4.71 us (3%)
  between operations  2.08 us (1%)
    pallas_call x1, Pallas kernels, body(): pl.pallas_call(kernel, out_shape=(sds(piece), sds(tile, F32), sds(tile, F...  144 us
    reshape x4, local copies, waits for them, and re-layouts, slots(): total.reshape(PAIRS, BLOCK, 2, BLOCK).transpose(0, 2, 1, 3)  3.4 us

profile of v2, /device:TPU:50, one launch (start us, length us, event | category | flops | bytes accessed | tf_op | source)
XLA Modules:
  0.0 161.2 jit_solution(7533538230556225299)
XLA Ops:
  1.9 0.0 copy-start.4
  1.9 0.6 copy-done.4
  2.6 0.1 pad_add_fusion.2
  2.7 0.1 pad.7.clone
  2.8 0.0 copy-start.3
  2.8 0.1 broadcast_compare_fusion
  2.9 0.6 copy-done.3
  3.5 0.1 copy.18
  3.6 0.1 copy.17
  3.7 0.2 fusion
  3.9 0.7 fusion.1.meta
  4.5 1.4 stack.14
  6.0 0.0 copy-start.1
  6.0 0.5 copy.15
  6.5 0.4 copy-done.1
  6.9 0.5 stack.15
  7.4 0.5 copy.16
  8.0 1.6 %maximum_bitcast_fusion = bf16[2,15,64,2,64]{4,3,2,1,0:T(2,128)(2,1)S(1)} fusion(bf16[1,15,2,64,64]{4,2,3,1,0:T(2,128)(2,1)S(1)} %copy.16, bf16[1,15,2,64,64]{4,2,3,1,0:T(2,128)(2,1)S(1)} %copy.15), kind=kLoop, calls=%fused_computation | loop fusion | flops 245760 | bytes 983040 | tf_op jit(solution)/shard_map/transpose | solution.py:541
  9.6 1.2 reshape.199.pay
  10.8 143.6 %layer.1 = (bf16[96,640]{1,0:T(8,128)(2,1)}, f32[960,128]{1,0:T(8,128)}, f32[960,128]{1,0:T(8,128)}) custom-call(bf16[96,640]{1,0:T(8,128)(2,1)} %tok.1, bf16[96,640]{1,0:T(8,128)(2,1)} %out.1, bf16[2,960,128]{2,1,0:T(8,128)(2,1)} %reshape.199.pay, s32[8,128]{1,0:T(8,128)} %fusion.1.meta), custom_call_target="tpu_custom_call" | custom-call | tf_op jit(solution)/shard_map/layer/pallas_call | solution.py:545
  154.5 1.6 reshape.200
  156.1 0.1 copy.19
  156.2 0.0 copy-start
  156.2 0.6 reshape.201
  156.8 0.4 copy-done
  157.2 0.6 reshape.202
  157.8 0.1 copy.20
  157.9 0.6 reshape.203
  158.5 0.0 copy-start.2
  158.6 2.0 %broadcast_select_fusion = (f32[1,1,30,4096]{3,1,2,0:T(1,128)}, f32[1,1,30,4096]{3,1,2,0:T(1,128)}) fusion(f32[1,1,30,4096]{3,1,2,0:T(1,128)S(1)} %reshape.203, pred[30]{0:T(512)(128)(4,1)S(1)} %iota_compare_fusion, f32[1,1,30,4096]{3,1,2,0:T(1,128)S(1)} %reshape.201, pred[30]{0:T(512)(128)(4,1)S(1)} %iota_compare_fusion.1), kind=kLoop, calls=%fused_computation.1 | loop fusion | flops 245760 | bytes 1966140 | tf_op jit(solution)/shard_map/jit(_where)/select_n | solution.py:591
  160.6 0.0 copy-done.2
  160.6 0.6 copy.24
  (9 shorter events, 0.1 us)
Async XLA Ops:
  1.9 0.7 copy-start.4
  2.8 0.7 copy-start.3
  6.0 1.0 copy-start.1
  156.2 1.0 copy-start
  158.5 2.0 %copy-start.2 = (bf16[96,640]{1,0:T(8,128)(2,1)S(1)}, bf16[96,640]{1,0:T(8,128)(2,1)}, u32[]{:S(2)}) copy-start(bf16[96,640]{1,0:T(8,128)(2,1)} %get-tuple-element.18) | copy-start | bytes 368644

commit v3 on v2

--- a/solution.py
+++ b/solution.py
@@ -104,6 +104,7 @@
         place.partner_hi(),
         place.along_y(1),
         place.along_y(-1),
+        place.along_y(2),
         place.along_z(1),
         place.along_z(-1),
         place.out_to(),
@@ -112,7 +113,7 @@
     barrier = pltpu.get_barrier_semaphore()
     for device in devices:
         pl.semaphore_signal(barrier, inc=1, device_id=device, device_id_type=MESH)
-    pl.semaphore_wait(barrier, len(devices))
+    return barrier, len(devices)
 
 
 def add(*parts):
@@ -123,26 +124,40 @@
 
 
 def kernel(
-    tok, out, pay, meta,
+    tok, out, meta, up_blocks, up_counts, down_blocks, down_counts,
     tok_out, up_out, down_out,
+    pay, wide, pairs,
     held, strip, numbers, numbers_sm, dense, blocks, pre, slope_part, hidden, pre_grad, grads,
     own_tok, core_send, from_core, tok_send, right_in, left_in, right_far, left_far, lo_out, lo_in, home,
-    part, y_far, y_right, y_left, y_send, hi_out, hi_in,
+    part, x_in, y_far, y_right, y_left, y_send, hi_out, hi_in,
     meta_sems, send_sems, recv_sems,
 ):
     place = Place()
     z, y, xh, xl, core = place.z, place.y, place.xh, place.xl, place.core
     mine, twin = place.p, y * 2 + 1 - xh
     right, left = place.along_y(1), place.along_y(-1)
-    greet(place)
+    barrier, greetings = greet(place)
+
+    for which, raw in enumerate((up_blocks, down_blocks)):
+        for k in range(BLOCK // 2):
+            wide[k, 0:CAP, :] = raw[0, 0, :, k * 128 : (k + 1) * 128].astype(F32)
+            even = wide[k, pl.ds(0, PAIRS, stride=2), :]
+            odd = wide[k, pl.ds(1, PAIRS, stride=2), :]
+            pairs[:, 2 * k, :] = jnp.concatenate([even[:, :BLOCK], odd[:, :BLOCK]], axis=1)
+            pairs[:, 2 * k + 1, :] = jnp.concatenate([even[:, BLOCK:], odd[:, BLOCK:]], axis=1)
+        pay[which] = pairs[...].reshape(ROWS, 128).astype(BF16)
+
+    pl.semaphore_wait(barrier, greetings)
     copies = Copies(send_sems, recv_sems)
     go = copies.start
 
+    def along_y(numbers_ref, tile_ref, tile):
+        return [
+            (go(numbers_ref, numbers.at[tile], device), go(tile_ref, strip.at[:, tile], device))
+            for device in (right, left, place.along_y(2))
+        ]
+
     perm_tok = go(tok, held.at[0, place.p, core, xl], place.out_to())
-    perm_out = go(out, held.at[1, place.p, core, xl], place.out_to())
-    swap_meta = go(meta, numbers.at[mine], place.partner_hi())
-    swap = go(pay, strip.at[:, mine], place.partner_hi())
-
     def to_scalars(source, tile, index):
         copy = pltpu.make_async_copy(source, numbers_sm.at[tile], meta_sems.at[index])
         copy.start()
@@ -194,38 +209,6 @@
 
     lo_outs, core_toks, core_outs = {}, {}, {}
 
-    perm_tok.wait_recv()
-    piece = held.at[0, place.f, core, xl]
-    lo_tok = go(piece, piece, place.partner_lo())
-    meta_right = go(meta, numbers.at[mine], right)
-    meta_left = go(meta, numbers.at[mine], left)
-    near = [
-        [go(pay.at[w], strip.at[w, mine], right), go(pay.at[w], strip.at[w, mine], left)] for w in range(2)
-    ]
-
-    lo_tok.wait_recv()
-    right_tok = go(toks(0), toks(0), place.along_z(1))
-    left_tok = go(toks(0), toks(0), place.along_z(-1))
-    core_toks[0] = to_core(toks(0))
-
-    swap_meta.wait_recv()
-    ref = numbers.at[twin]
-    twin_meta_right = go(ref, ref, right)
-    twin_meta_left = go(ref, ref, left)
-    twin_scalars = to_scalars(ref, twin, 1)
-    swap.wait_recv()
-    near_twin = []
-    for w in range(2):
-        ref = strip.at[w, twin]
-        near_twin.append([go(ref, ref, right), go(ref, ref, left)])
-    twin_scalars.wait()
-    lax.fori_loop(0, 2, fill_tiles(lambda index: twin), 0)
-
-    perm_out.wait_recv()
-    right_out = go(outs(0), outs(0), place.along_z(1))
-    left_out = go(outs(0), outs(0), place.along_z(-1))
-    lo_outs[0] = go(outs(0), outs(0), place.partner_lo())
-
     def tile_at(step, side):
         return ((y + step + 4) % 4) * 2 + (xh + side) % 2
 
@@ -241,8 +224,41 @@
             core_toks[step].wait_recv()
             core_outs[step].wait_recv()
 
-    far_copies = []
-    for step in (1, 2, 3, 4):
+    perm_tok.wait_recv()
+    piece = held.at[0, place.f, core, xl]
+    lo_tok = go(piece, piece, place.partner_lo())
+    swap_meta = go(meta, numbers.at[mine], place.partner_hi())
+    swap = go(pay, strip.at[:, mine], place.partner_hi())
+
+    lo_tok.wait_recv()
+    right_tok = go(toks(0), toks(0), place.along_z(1))
+    left_tok = go(toks(0), toks(0), place.along_z(-1))
+    core_toks[0] = to_core(toks(0))
+    perm_out = go(out, held.at[1, place.p, core, xl], place.out_to())
+    y_own = along_y(meta, pay, mine)
+
+    swap_meta.wait_recv()
+    twin_scalars = to_scalars(numbers.at[twin], twin, 1)
+    swap.wait_recv()
+    y_twin = along_y(numbers.at[twin], strip.at[:, twin], twin)
+    twin_scalars.wait()
+
+    def tok_step(step):
+        nonlocal right_tok, left_tok
+        right_tok.wait_recv()
+        ref = toks(-step)
+        if step < 4:
+            right_tok = go(ref, ref, place.along_z(1))
+        core_toks[4 if step == 4 else -step] = to_core(ref)
+        if step < 4:
+            left_tok.wait_recv()
+            ref = toks(step)
+            if step < 3:
+                left_tok = go(ref, ref, place.along_z(-1))
+            core_toks[step] = to_core(ref)
+
+    def out_step(step):
+        nonlocal right_out, left_out
         if step < 4:
             right_out.wait_recv()
             ref = outs(-step)
@@ -255,65 +271,54 @@
             left_out = go(ref, ref, place.along_z(-1))
         lo_outs[step] = go(ref, ref, place.partner_lo())
 
-        right_tok.wait_recv()
-        ref = toks(-step)
-        if step < 4:
-            right_tok = go(ref, ref, place.along_z(1))
-        core_toks[-step] = to_core(ref)
-        if step < 4:
-            left_tok.wait_recv()
-            ref = toks(step)
-            if step < 3:
-                left_tok = go(ref, ref, place.along_z(-1))
-            core_toks[step] = to_core(ref)
-        if step == 4:
-            core_toks[4] = core_toks[-4]
-
-        if step in (1, 2):
-            side = step - 1
-            came, met = (near, (meta_right, meta_left)) if side == 0 else (near_twin, (twin_meta_right, twin_meta_left))
-            from_left, from_right = tile_at(-1, side), tile_at(1, side)
-            met[0].wait_recv()
-            far_meta = go(numbers.at[from_left], numbers.at[from_left], right)
-            scalars = [to_scalars(numbers.at[from_left], from_left, 2 + 3 * side)]
-            met[1].wait_recv()
-            scalars.append(to_scalars(numbers.at[from_right], from_right, 3 + 3 * side))
-            came[0][0].wait_recv()
-            ref = strip.at[0, from_left]
-            far_up = go(ref, ref, right)
-            came[1][1].wait_recv()
-            ref = strip.at[1, from_right]
-            far_down = go(ref, ref, left)
-            came[0][1].wait_recv()
-            came[1][0].wait_recv()
-            for copy in scalars:
-                copy.wait()
-            far_copies.append((far_meta, far_up, far_down))
-            lax.fori_loop(0, 4, fill_tiles(lambda index, side=side: tile_at(2 * index - 1, side)), 0)
-        for done in ((0,), (-1, 1), (-2, 2), (-3, 3))[step - 1]:
-            lo_outs[done].wait_recv()
-            core_outs[done] = to_core(both_outs(done))
-        if step == 3:
-            scalars = []
-            for side in range(2):
-                tile = tile_at(2, side)
-                far_copies[side][0].wait_recv()
-                scalars.append(to_scalars(numbers.at[tile], tile, 4 + 3 * side))
-            for side in range(2):
-                far_copies[side][1].wait_recv()
-                far_copies[side][2].wait_recv()
-            for copy in scalars:
-                copy.wait()
-            lax.fori_loop(0, 4, fill_tiles(lambda index: tile_at(2, index)), 0)
-            multiply_ready((0, -1, 1))
-
-            def near_features(index, carry):
-                multiply(index - 1)
-                return carry
-
-            lax.fori_loop(0, 3, near_features, 0)
-    lo_outs[4].wait_recv()
-    core_outs[4] = to_core(both_outs(4))
+    def outs_to_core(steps):
+        for step in steps:
+            lo_outs[step].wait_recv()
+            core_outs[step] = to_core(both_outs(step))
+
+    def out_begin():
+        perm_out.wait_recv()
+        lo_outs[0] = go(outs(0), outs(0), place.partner_lo())
+        return go(outs(0), outs(0), place.along_z(1)), go(outs(0), outs(0), place.along_z(-1))
+
+    def tiles_came(came, side, first):
+        scalars = []
+        for number, step in enumerate((-1, 1, 2)):
+            came[number][0].wait_recv()
+            scalars.append(to_scalars(numbers.at[tile_at(step, side)], tile_at(step, side), first + number))
+        for number in range(3):
+            came[number][1].wait_recv()
+            scalars[number].wait()
+
+    def fill_along_y(side):
+        lax.fori_loop(0, 6, fill_tiles(lambda index: tile_at(index + 1, side)), 0)
+
+    tok_step(1)
+    lax.fori_loop(0, 2, fill_tiles(lambda index: twin), 0)
+    right_out, left_out = out_begin()
+    tok_step(2)
+    out_step(1)
+    outs_to_core((0,))
+    tok_step(3)
+    out_step(2)
+    outs_to_core((-1, 1))
+    tok_step(4)
+    out_step(3)
+    outs_to_core((-2, 2))
+    tiles_came(y_own, 0, 2)
+    fill_along_y(0)
+    out_step(4)
+    outs_to_core((-3, 3))
+    tiles_came(y_twin, 1, 5)
+    fill_along_y(1)
+    multiply_ready((0, -1, 1))
+
+    def near_features(index, carry):
+        multiply(index - 1)
+        return carry
+
+    lax.fori_loop(0, 3, near_features, 0)
+    outs_to_core((4,))
     multiply_ready((-2, 2, -3, 3))
 
     def late_features(index, carry):
@@ -387,39 +392,33 @@
                 core_send.at[f], from_core.at[f], place.sibling(), core_first + first + number
             )
 
-    def far_tiles(index, carry):
+    x_steps = (2, 1, -1, 0)
+    x_first = copies.reserve(4)
+    far_first = copies.reserve(2)
+    near_first = copies.reserve(2)
+
+    def x_send(slot, tile):
+        up_tile(tile)
+        copies.copy(part.at[0, tile], x_in.at[slot], place.partner_hi(), x_first + slot).start()
+
+    def early_tiles(index, carry):
+        x_send(index, tile_at(2 - index, 1))
         tile = tile_at(2, 1 - index)
-        up_tile(tile)
-        copies.copy(part.at[0, tile], y_far.at[0, 1 - index], right, far_first + index).start()
         down_tile(tile)
-        copies.copy(part.at[1, tile], y_far.at[1, 1 - index], left, far_first + 2 + index).start()
-        return carry
-
-    far_first = copies.reserve(4)
-    lax.fori_loop(0, 2, far_tiles, 0)
-    far_in = [
-        [copies.started(part.at[0, tile_at(2, side)], y_far.at[0, side], right, far_first + 1 - side) for side in range(2)],
-        [copies.started(part.at[1, tile_at(2, side)], y_far.at[1, side], left, far_first + 3 - side) for side in range(2)],
-    ]
-
-    tok_features(0, (4, 3, -3), lambda index: 4 - index + (index // 2) * 3)
-
-    def near_tiles(index, carry):
+        copies.copy(part.at[1, tile], y_far.at[1, 1 - index], left, far_first + index).start()
+        return carry
+
+    def next_tiles(index, carry):
+        x_send(2 + index, tile_at(index - 1, 1))
         tile = tile_at(1, 1 - index)
         down_tile(tile)
         copies.copy(part.at[1, tile], y_right.at[1, 1 - index], right, near_first + index).start()
-        tile = tile_at(-1, 1 - index)
-        up_tile(tile)
-        copies.copy(part.at[0, tile], y_left.at[0, 1 - index], left, near_first + 2 + index).start()
-        return carry
-
-    near_first = copies.reserve(4)
-    lax.fori_loop(0, 2, near_tiles, 0)
-    down_right = [
-        copies.started(part.at[1, tile_at(1, side)], y_right.at[1, side], right, near_first + 1 - side) for side in range(2)
-    ]
-    up_left = [
-        copies.started(part.at[0, tile_at(-1, side)], y_left.at[0, side], left, near_first + 3 - side) for side in range(2)
+        return carry
+
+    tok_features(0, (4, 3, -3), lambda index: 4 - index + (index // 2) * 3)
+    lax.fori_loop(0, 2, early_tiles, 0)
+    far_down = [
+        copies.started(part.at[1, tile_at(2, side)], y_far.at[1, side], left, far_first + 1 - side) for side in range(2)
     ]
 
     f = place.feature(4)
@@ -428,7 +427,14 @@
     go_right = go(tok_send.at[0, 0], right_far, place.along_z(1))
     go_left = go(tok_send.at[0, 1], left_far, place.along_z(-1))
 
-    tok_features(3, (2, -2), lambda index: 2 + 4 * index)
+    lax.fori_loop(0, 2, next_tiles, 0)
+    down_right = [
+        copies.started(part.at[1, tile_at(1, side)], y_right.at[1, side], right, near_first + 1 - side) for side in range(2)
+    ]
+    from_twin = {
+        step: copies.started(part.at[0, tile_at(step, 1)], x_in.at[slot], place.partner_hi(), x_first + slot)
+        for slot, step in enumerate(x_steps)
+    }
 
     def pass_on(step):
         nonlocal go_right, go_left
@@ -453,42 +459,62 @@
         go_left = go(tok_send.at[slot + 1], left_in.at[3 - step], place.along_z(-1))
 
     pass_on(3)
-
-    def up_more(index, carry):
-        up_tile(tile_at(1, 1 - index))
+    tok_features(3, (2, -2), lambda index: 2 + 4 * index)
+
+    def more_tiles(index, carry):
+        up_tile(tile_at(2 + index, 0))
         down_tile(tile_at(-1, 1 - index))
         return carry
 
-    lax.fori_loop(0, 2, up_more, 0)
-    up_right, down_left = [None, None], [None, None]
+    lax.fori_loop(0, 2, more_tiles, 0)
+    from_twin[2].wait_recv()
+    y_send[0, 0] = add(part[0, tile_at(2, 0)], x_in[0]).astype(BF16)
+    far_up = go(y_send.at[0, 0], y_far.at[0, 0], right)
+    down_left = [None, None]
     for side in (1, 0):
-        far_in[0][side].wait_recv()
-        y_send[0, side] = add(part[0, tile_at(1, side)], y_far[0, side]).astype(BF16)
-        up_right[side] = go(y_send.at[0, side], y_right.at[0, side], right)
-        far_in[1][side].wait_recv()
+        far_down[side].wait_recv()
         y_send[1, side] = add(part[1, tile_at(-1, side)], y_far[1, side]).astype(BF16)
         down_left[side] = go(y_send.at[1, side], y_left.at[1, side], left)
+    pass_on(2)
+    from_twin[-1].wait_recv()
+    y_send[0, 1] = add(part[0, tile_at(-1, 0)], x_in[2]).astype(BF16)
+    up_left = go(y_send.at[0, 1], y_left.at[0, 0], left)
 
     tok_features(5, (1, -1, 0), lambda index: 1 + 6 * index - (index // 2) * 5)
-    pass_on(2)
-
-    def own_tiles(index, carry):
-        up_tile(tile_at(0, 1 - index))
+
+    def last_tiles(index, carry):
+        up_tile(tile_at(1 - index, 0))
         down_tile(tile_at(0, 1 - index))
         return carry
 
-    lax.fori_loop(0, 2, own_tiles, 0)
+    lax.fori_loop(0, 2, last_tiles, 0)
+    from_twin[1].wait_recv()
+    far_up.wait_recv()
+    y_send[0, 2] = add(part[0, tile_at(1, 0)], x_in[1], y_far[0, 0]).astype(BF16)
+    up_right = go(y_send.at[0, 2], y_right.at[0, 0], right)
     pass_on(1)
 
-    hi = []
-    up_left[1].wait_recv()
-    up_right[1].wait_recv()
-    hi_out[0] = add(part[0, twin], y_left[0, 1], y_right[0, 1]).astype(BF16)
-    hi.append(go(hi_out.at[0], hi_in.at[0], place.partner_hi()))
     down_left[1].wait_recv()
     down_right[1].wait_recv()
-    hi_out[1] = add(part[1, twin], y_left[1, 1], y_right[1, 1]).astype(BF16)
-    hi.append(go(hi_out.at[1], hi_in.at[1], place.partner_hi()))
+    hi_out[...] = add(part[1, twin], y_left[1, 1], y_right[1, 1]).astype(BF16)
+    hi = go(hi_out, hi_in, place.partner_hi())
+
+    def put(target, total, counts):
+        pairs[...] = total.reshape(PAIRS, BLOCK, 128)
+        slot = 2 * lax.broadcasted_iota(jnp.int32, (PAIRS, 128), 0)
+        even_live, odd_live = slot < counts[0, 0], slot + 1 < counts[0, 0]
+        for k in range(BLOCK // 2):
+            low, high = pairs[:, 2 * k, :], pairs[:, 2 * k + 1, :]
+            even = jnp.concatenate([low[:, :BLOCK], high[:, :BLOCK]], axis=1)
+            odd = jnp.concatenate([low[:, BLOCK:], high[:, BLOCK:]], axis=1)
+            wide[k, pl.ds(0, PAIRS, stride=2), :] = jnp.where(even_live, even, 0.0)
+            wide[k, pl.ds(1, PAIRS, stride=2), :] = jnp.where(odd_live, odd, 0.0)
+            target[0, 0, :, k * 128 : (k + 1) * 128] = wide[k, 0:CAP, :]
+
+    from_twin[0].wait_recv()
+    up_left.wait_recv()
+    up_right.wait_recv()
+    put(up_out, add(part[0, mine], x_in[3], y_left[0, 0], y_right[0, 0]), up_counts)
 
     f = place.f
     core_in[0].wait_recv()
@@ -497,20 +523,21 @@
     other = 1 - xl
     lo_out[...] = add(own_tok[f, other], from_core[f, other], right_in[2, other], left_in[2, other]).astype(BF16)
     lo = go(lo_out, lo_in, place.partner_lo())
+
+    down_left[0].wait_recv()
+    down_right[0].wait_recv()
     lo.wait_recv()
     home[...] = add(own_tok[f, xl], from_core[f, xl], right_in[2, xl], left_in[2, xl], lo_in[...]).astype(BF16)
     back = go(home, tok_out, place.back_to())
 
-    for which, outputs, first, second in ((0, up_out, up_left, up_right), (1, down_out, down_left, down_right)):
-        first[0].wait_recv()
-        second[0].wait_recv()
-        hi[which].wait_recv()
-        outputs[...] = add(part[which, mine], y_left[which, 0], y_right[which, 0], hi_in[which])
+    hi.wait_recv()
+    put(down_out, add(part[1, mine], y_left[1, 0], y_right[1, 0], hi_in[...]), down_counts)
     back.wait_recv()
     copies.finish()
-
-
-COPIES = 93
+    assert copies.number == COPIES, copies.number
+
+
+COPIES = 87
 
 
 def vmem(count):
@@ -537,17 +564,19 @@
 
 
 def body(tokens, up_blocks, up_layout, up_counts, down_blocks, down_layout, down_counts, grad_out):
-    pay = jnp.stack([up_blocks[0, 0], down_blocks[0, 0]]).reshape(2, PAIRS, 2, BLOCK, BLOCK)
-    pay = pay.transpose(0, 1, 3, 2, 4).reshape(2, ROWS, 2 * BLOCK)
     meta = offsets(up_layout, up_counts, down_layout, down_counts)
     tile = (ROWS, 128)
+    scalar = [pl.BlockSpec(memory_space=pltpu.SMEM)]
     piece = (TOK, FEAT)
-    tok_grad, up_sum, down_sum = pl.pallas_call(
+    return pl.pallas_call(
         kernel,
-        out_shape=(sds(piece), sds(tile, F32), sds(tile, F32)),
-        in_specs=vmem(4),
+        out_shape=(sds(piece), sds((1, 1, CAP, BLOCK * BLOCK), F32), sds((1, 1, CAP, BLOCK * BLOCK), F32)),
+        in_specs=vmem(4) + scalar + vmem(1) + scalar,
         out_specs=tuple(vmem(3)),
         scratch_shapes=[
+            pltpu.VMEM((2,) + tile, BF16),
+            pltpu.VMEM((BLOCK // 2, CAP + 2, 128), F32),
+            pltpu.VMEM((PAIRS, BLOCK, 128), F32),
             pltpu.VMEM((2, 8, 2, 2) + piece, BF16),
             pltpu.VMEM((2, 8) + tile, BF16),
             pltpu.VMEM((8, 8, 128), jnp.int32),
@@ -571,26 +600,20 @@
             pltpu.VMEM(piece, BF16),
             pltpu.VMEM(piece, BF16),
             pltpu.VMEM((2, 8) + tile, BF16),
+            pltpu.VMEM((4,) + tile, BF16),
             pltpu.VMEM((2, 2) + tile, BF16),
             pltpu.VMEM((2, 2) + tile, BF16),
             pltpu.VMEM((2, 2) + tile, BF16),
-            pltpu.VMEM((2, 2) + tile, BF16),
-            pltpu.VMEM((2,) + tile, BF16),
-            pltpu.VMEM((2,) + tile, BF16),
+            pltpu.VMEM((2, 3) + tile, BF16),
+            pltpu.VMEM(tile, BF16),
+            pltpu.VMEM(tile, BF16),
             pltpu.SemaphoreType.DMA((8,)),
             pltpu.SemaphoreType.DMA((COPIES,)),
             pltpu.SemaphoreType.DMA((COPIES,)),
         ],
         compiler_params=pltpu.CompilerParams(collective_id=0, has_side_effects=True, vmem_limit_bytes=60 * 2**20),
         name="layer",
-    )(tokens, grad_out, pay, meta)
-
-    def slots(total, counts):
-        flat = total.reshape(PAIRS, BLOCK, 2, BLOCK).transpose(0, 2, 1, 3).reshape(CAP, BLOCK * BLOCK)
-        live = jnp.arange(CAP, dtype=jnp.int32) < counts[0, 0]
-        return jnp.where(live[:, None], flat, 0.0)[None, None]
-
-    return tok_grad, slots(up_sum, up_counts), slots(down_sum, down_counts)
+    )(tokens, grad_out, meta, up_blocks, up_counts, down_blocks, down_counts)
 
 
 def solution(mesh):

time: 161 us -> 149 us (0.925)
  the two profiles are of different devices: /device:TPU:50 before, /device:TPU:48 now
where the time goes in v3:
time: 149 us; the launch traced here: 148 us
  Pallas kernels  140 us (94%)
  local copies, waits for them, and re-layouts  5.84 us (4%)
  between operations  1.97 us (1%)
    pallas_call x1, Pallas kernels, body(): pl.pallas_call(kernel, out_shape=(sds(piece), sds((1, 1, CAP, BLOCK * BLO...  140 us
    pallas_call x2, local copies, waits for them, and re-layouts, body(): pl.pallas_call(kernel, out_shape=(sds(piece), sds((1, 1, CAP, BLOCK * BLO...  3.67 us

profile of v3, /device:TPU:48, one launch (start us, length us, event | category | flops | bytes accessed | tf_op | source)
XLA Modules:
  0.0 148.5 jit_solution(12305591224847624215)
XLA Ops:
  1.9 0.0 copy-start.3
  1.9 0.6 copy-done.3
  2.6 0.1 pad_add_fusion.2
  2.7 0.1 pad.7.clone
  2.8 0.0 copy-start.2
  2.8 0.1 broadcast_compare_fusion
  2.9 0.6 copy-done.2
  3.5 0.1 copy.14
  3.6 0.1 copy.13
  3.7 0.2 fusion
  3.9 0.7 fusion.1.meta
  4.5 139.6 %layer.1 = (bf16[96,640]{1,0:T(8,128)(2,1)}, f32[1,1,30,4096]{3,2,1,0:T(8,128)}, f32[1,1,30,4096]{3,2,1,0:T(8,128)}) custom-call(bf16[96,640]{1,0:T(8,128)(2,1)} %tok.1, bf16[96,640]{1,0:T(8,128)(2,1)} %out.1, s32[8,128]{1,0:T(8,128)} %fusion.1.meta, bf16[1,1,30,4096]{3,2,1,0:T(8,128)(2,1)} %up_blocks.1, s32[1,1]{1,0:T(1,128)} %copy.18.up_counts, ...), custom_call_target="tpu_custom_call" | custom-call | tf_op jit(solution)/shard_map/layer/pallas_call | solution.py:571
  144.1 0.0 copy-start
  144.2 2.4 %copy.15 = f32[1,1,30,4096]{3,1,2,0:T(1,128)} copy(f32[1,1,30,4096]{3,2,1,0:T(8,128)} %get-tuple-element.7) | data formatting | bytes 983040 | tf_op jit(solution)/shard_map/layer/pallas_call | solution.py:571
  146.5 0.0 copy-done
  146.5 0.0 copy-start.1
  146.5 1.3 copy.16
  147.8 0.0 copy-done.1
  147.8 0.6 copy.20
  (7 shorter events, 0.1 us)
Async XLA Ops:
  1.9 0.7 copy-start.3
  2.8 0.7 copy-start.2
  144.1 2.4 %copy-start = (f32[1,1,30,4096]{3,2,1,0:T(8,128)S(1)}, f32[1,1,30,4096]{3,2,1,0:T(8,128)}, u32[]{:S(2)}) copy-start(f32[1,1,30,4096]{3,2,1,0:T(8,128)} %get-tuple-element.8) | copy-start | bytes 1474564
  146.5 1.3 copy-start.1

commit v4 on v3

--- a/solution.py
+++ b/solution.py
@@ -226,13 +226,20 @@
 
     perm_tok.wait_recv()
     piece = held.at[0, place.f, core, xl]
+
+    def tok_pass(step, part_of, device):
+        ref = held.at[0, place.feature(step), core, (xl + part_of) % 2]
+        return go(ref, ref, device)
+
     lo_tok = go(piece, piece, place.partner_lo())
+    right_tok = [tok_pass(0, 0, place.along_z(1))]
+    left_tok = [tok_pass(0, 0, place.along_z(-1))]
     swap_meta = go(meta, numbers.at[mine], place.partner_hi())
     swap = go(pay, strip.at[:, mine], place.partner_hi())
 
     lo_tok.wait_recv()
-    right_tok = go(toks(0), toks(0), place.along_z(1))
-    left_tok = go(toks(0), toks(0), place.along_z(-1))
+    right_tok.append(tok_pass(0, 1, place.along_z(1)))
+    left_tok.append(tok_pass(0, 1, place.along_z(-1)))
     core_toks[0] = to_core(toks(0))
     perm_out = go(out, held.at[1, place.p, core, xl], place.out_to())
     y_own = along_y(meta, pay, mine)
@@ -244,18 +251,17 @@
     twin_scalars.wait()
 
     def tok_step(step):
-        nonlocal right_tok, left_tok
-        right_tok.wait_recv()
-        ref = toks(-step)
+        for part_of in range(2):
+            right_tok[part_of].wait_recv()
+            if step < 4:
+                right_tok[part_of] = tok_pass(-step, part_of, place.along_z(1))
+            if step < 4:
+                left_tok[part_of].wait_recv()
+            if step < 3:
+                left_tok[part_of] = tok_pass(step, part_of, place.along_z(-1))
+        core_toks[4 if step == 4 else -step] = to_core(toks(-step))
         if step < 4:
-            right_tok = go(ref, ref, place.along_z(1))
-        core_toks[4 if step == 4 else -step] = to_core(ref)
-        if step < 4:
-            left_tok.wait_recv()
-            ref = toks(step)
-            if step < 3:
-                left_tok = go(ref, ref, place.along_z(-1))
-            core_toks[step] = to_core(ref)
+            core_toks[step] = to_core(toks(step))
 
     def out_step(step):
         nonlocal right_out, left_out
@@ -537,7 +543,7 @@
     assert copies.number == COPIES, copies.number
 
 
-COPIES = 87
+COPIES = 94
 
 
 def vmem(count):

time: 149 us -> 149 us (level)
  no operation moved by 1% of the time
where the time goes in v4:
time: 149 us
  Pallas kernels  140 us (94%)
  local copies, waits for them, and re-layouts  5.84 us (4%)
  between operations  1.97 us (1%)
    pallas_call x1, Pallas kernels, body(): pl.pallas_call(kernel, out_shape=(sds(piece), sds((1, 1, CAP, BLOCK * BLO...  140 us
    pallas_call x2, local copies, waits for them, and re-layouts, body(): pl.pallas_call(kernel, out_shape=(sds(piece), sds((1, 1, CAP, BLOCK * BLO...  3.67 us

profile of v4, /device:TPU:48, one launch (start us, length us, event | category | flops | bytes accessed | tf_op | source)
XLA Modules:
  0.0 149.0 jit_solution(729804059884065312)
XLA Ops:
  1.9 0.0 copy-start.3
  1.9 0.6 copy-done.3
  2.6 0.1 pad_add_fusion.2
  2.7 0.1 pad.7.clone
  2.8 0.0 copy-start.2
  2.8 0.1 broadcast_compare_fusion
  2.9 0.6 copy-done.2
  3.5 0.1 copy.14
  3.6 0.1 copy.13
  3.7 0.2 fusion
  3.9 0.7 fusion.1.meta
  4.5 140.1 %layer.1 = (bf16[96,640]{1,0:T(8,128)(2,1)}, f32[1,1,30,4096]{3,2,1,0:T(8,128)}, f32[1,1,30,4096]{3,2,1,0:T(8,128)}) custom-call(bf16[96,640]{1,0:T(8,128)(2,1)} %tok.1, bf16[96,640]{1,0:T(8,128)(2,1)} %out.1, s32[8,128]{1,0:T(8,128)} %fusion.1.meta, bf16[1,1,30,4096]{3,2,1,0:T(8,128)(2,1)} %up_blocks.1, s32[1,1]{1,0:T(1,128)} %copy.18.up_counts, ...), custom_call_target="tpu_custom_call" | custom-call | tf_op jit(solution)/shard_map/layer/pallas_call | solution.py:577
  144.6 0.0 copy-start
  144.6 2.4 %copy.15 = f32[1,1,30,4096]{3,1,2,0:T(1,128)} copy(f32[1,1,30,4096]{3,2,1,0:T(8,128)} %get-tuple-element.7) | data formatting | bytes 983040 | tf_op jit(solution)/shard_map/layer/pallas_call | solution.py:577
  147.0 0.0 copy-done
  147.0 0.0 copy-start.1
  147.0 1.3 copy.16
  148.3 0.0 copy-done.1
  148.3 0.6 copy.20
  (7 shorter events, 0.1 us)
Async XLA Ops:
  1.9 0.7 copy-start.3
  2.8 0.7 copy-start.2
  144.6 2.4 %copy-start = (f32[1,1,30,4096]{3,2,1,0:T(8,128)S(1)}, f32[1,1,30,4096]{3,2,1,0:T(8,128)}, u32[]{:S(2)}) copy-start(f32[1,1,30,4096]{3,2,1,0:T(8,128)} %get-tuple-element.8) | copy-start | bytes 1474564
  147.0 1.3 copy-start.1
